TPU v7x, 32 devices: a whole 2x2x4 slice. The times are simulated.
32 devices in a mesh: prefix: 4 (over z), group: 4 (over y, core), tensor: 2 (over x).
Axes of the slice: x: 2, y: 2, z: 4, core: 2. Of those that a mesh axis runs over, the one named last changes fastest.
Arguments:
- resp_query: bfloat16 [512, 8, 32, 128], P('prefix', 'group', 'tensor'), may hold values from -6 to 6
- response_key: bfloat16 [512, 8, 4, 128], P('prefix', 'group', 'tensor'), may hold values from -6 to 6
- response_value: bfloat16 [512, 8, 4, 128], P('prefix', 'group', 'tensor'), may hold values from -6 to 6
- resp_cotangent: bfloat16 [512, 8, 32, 128], P('prefix', 'group', 'tensor'), may hold values from -300 to 300
- prompt_key: bfloat16 [256, 4, 128], P('prefix', 'tensor'), may hold values from -6.2 to 6.2
- prompt_value_rows: bfloat16 [256, 4, 128], P('prefix', 'tensor'), may hold values from -6 to 6
- key_matrix: bfloat16 [5120, 512], P(None, 'tensor'), may hold values from -0.078125 to 0.078125
- value_matrix: bfloat16 [5120, 512], P(None, 'tensor'), may hold values from -0.078125 to 0.078125
- resp_lengths: int32 [8], replicated, may hold values from 128 to 512, as said below
Outputs:
- resp_query_grad: bfloat16 [512, 8, 32, 128], P('prefix', 'group', 'tensor')
- resp_key_grad: bfloat16 [512, 8, 4, 128], P('prefix', 'group', 'tensor')
- resp_value_grad: bfloat16 [512, 8, 4, 128], P('prefix', 'group', 'tensor')
- prompt_input_grad: bfloat16 [256, 5120], P('prefix', 'tensor')
Inputs may be any that keep to these rules, and one draw needn't show every extreme that they name: `resp_lengths`: some response has all 512 tokens and another 512 // 4 in every draw.
All inputs are finite; a program needn't handle non-finite values.
Results may differ from a plain program's by a relative error of at most 0.0058.
Values may be sent and summed in bfloat16 or wider, within the bound.
A program may use at most 128 MiB of HBM per device.

v0:
```python
import math

import jax
import jax.numpy as jnp
from jax import lax
from jax.sharding import PartitionSpec as P

masked_score = -1e30
prompt_forms = ("lrkge,mke->rkglm", "rkglm,lrkge->mke", "rkglm,mke->lrkge")
causal_forms = ("lrkge,mrke->rkglm", "rkglm,lrkge->mrke", "rkglm,mrke->lrkge")


def block_length(total_rows, causal):
    wanted = 128 if causal else 512
    return wanted if total_rows % wanted == 0 else total_rows


def per_device(
    resp_query,
    response_key,
    response_value,
    resp_cotangent,
    prompt_key,
    prompt_value_rows,
    key_matrix,
    value_matrix,
    resp_lengths,
):
    query_rows, resp_count, query_heads, head_width = resp_query.shape
    kv_heads = response_key.shape[2]
    group_factor = query_heads // kv_heads
    prompt_rows = prompt_key.shape[0]
    score_scale = 1.0 / math.sqrt(head_width)
    prefix_index = lax.axis_index("prefix")
    offset = prefix_index * query_rows
    queries = resp_query.reshape(query_rows, resp_count, kv_heads, group_factor, head_width)
    query_pos = offset + jnp.arange(query_rows, dtype=jnp.int32)
    own_lengths = lax.dynamic_slice_in_dim(
        resp_lengths, lax.axis_index("group") * resp_count, resp_count
    )
    live_rows = query_pos[:, None] < own_lengths[None, :]
    cotangent = jnp.where(
        live_rows[:, :, None, None], resp_cotangent, jnp.zeros_like(resp_cotangent)
    )
    cotangent = cotangent.reshape(query_rows, resp_count, kv_heads, group_factor, head_width)
    all_pkeys, all_pvalues, all_rkeys, all_rvalues = (
        lax.all_gather(prompt_key, "prefix", axis=0, tiled=True),
        lax.all_gather(prompt_value_rows, "prefix", axis=0, tiled=True),
        lax.all_gather(response_key, "prefix", axis=0, tiled=True),
        lax.all_gather(response_value, "prefix", axis=0, tiled=True),
    )

    def score_block(key_block, causal, block_start):
        einsum_forms = causal_forms if causal else prompt_forms
        scores = (
            jnp.einsum(einsum_forms[0], queries, key_block, preferred_element_type=jnp.float32)
            * score_scale
        )
        if causal:
            key_pos = block_start + jnp.arange(key_block.shape[0], dtype=jnp.int32)
            visible = key_pos[None, :] <= query_pos[:, None]
            scores = jnp.where(visible, scores, masked_score)
        return scores

    def sweep_keys(step, state, keys, value_rows, causal):
        block_rows = block_length(keys.shape[0], causal)
        block_count = keys.shape[0] // block_rows
        key_stack = keys.reshape((block_count, block_rows) + keys.shape[1:])
        value_stack = value_rows.reshape((block_count, block_rows) + value_rows.shape[1:])
        block_starts = jnp.arange(block_count, dtype=jnp.int32) * block_rows

        def advance(current, pieces):
            key_block, value_block, block_start = pieces
            return step(current, key_block, value_block, causal, block_start)

        return lax.scan(advance, state, (key_stack, value_stack, block_starts))

    def stats_step(state, key_block, value_block, causal, block_start):
        running_max, running_sum = state
        scores = score_block(key_block, causal, block_start)
        new_max = jnp.maximum(running_max, jnp.max(scores, axis=-1))
        running_sum = running_sum * jnp.exp(running_max - new_max) + jnp.sum(
            jnp.exp(scores - new_max[..., None]), axis=-1
        )
        return ((new_max, running_sum), None)

    stat_shape = (resp_count, kv_heads, group_factor, query_rows)
    stats = (jnp.full(stat_shape, masked_score, jnp.float32), jnp.zeros(stat_shape, jnp.float32))
    stats, unused = sweep_keys(stats_step, stats, all_pkeys, all_pvalues, False)
    stats, unused = sweep_keys(stats_step, stats, all_rkeys, all_rvalues, True)
    log_total = stats[0] + jnp.log(stats[1])

    def prob_block(key_block, value_block, causal, block_start):
        einsum_forms = causal_forms if causal else prompt_forms
        scores = score_block(key_block, causal, block_start)
        attn_prob = jnp.exp(scores - log_total[..., None])
        attn_dprob = jnp.einsum(
            einsum_forms[0], cotangent, value_block, preferred_element_type=jnp.float32
        )
        return (attn_prob, attn_dprob)

    def delta_step(state, key_block, value_block, causal, block_start):
        attn_prob, attn_dprob = prob_block(key_block, value_block, causal, block_start)
        return (state + jnp.sum(attn_prob * attn_dprob, axis=-1), None)

    row_delta = jnp.zeros(stat_shape, jnp.float32)
    row_delta, unused = sweep_keys(delta_step, row_delta, all_pkeys, all_pvalues, False)
    row_delta, unused = sweep_keys(delta_step, row_delta, all_rkeys, all_rvalues, True)

    def grad_step(state, key_block, value_block, causal, block_start):
        einsum_forms = causal_forms if causal else prompt_forms
        attn_prob, attn_dprob = prob_block(key_block, value_block, causal, block_start)
        attn_dscore = (attn_prob * (attn_dprob - row_delta[..., None])).astype(jnp.bfloat16)
        prob_low = attn_prob.astype(jnp.bfloat16)
        value_sum = jnp.einsum(
            einsum_forms[1], prob_low, cotangent, preferred_element_type=jnp.float32
        )
        key_sum = (
            jnp.einsum(einsum_forms[1], attn_dscore, queries, preferred_element_type=jnp.float32)
            * score_scale
        )
        state = state + jnp.einsum(
            einsum_forms[2], attn_dscore, key_block, preferred_element_type=jnp.float32
        )
        return (state, jnp.stack((key_sum, value_sum), axis=2 if causal else 1))

    query_acc = jnp.zeros((query_rows, resp_count, kv_heads, group_factor, head_width), jnp.float32)
    query_acc, prompt_terms = sweep_keys(grad_step, query_acc, all_pkeys, all_pvalues, False)
    query_acc, resp_terms = sweep_keys(grad_step, query_acc, all_rkeys, all_rvalues, True)
    prompt_terms = prompt_terms.reshape((-1,) + prompt_terms.shape[2:])
    resp_terms = resp_terms.reshape((-1,) + resp_terms.shape[2:])
    query_grad = (
        (query_acc * score_scale)
        .astype(jnp.bfloat16)
        .reshape(query_rows, resp_count, query_heads, head_width)
    )
    prompt_share = lax.psum_scatter(prompt_terms, "prefix", scatter_dimension=0, tiled=True)
    prompt_share = lax.psum(prompt_share, "group")
    prompt_keys_grad = (
        prompt_share[:, 0].astype(jnp.bfloat16).reshape(prompt_rows, kv_heads * head_width)
    )
    prompt_values_grad = (
        prompt_share[:, 1].astype(jnp.bfloat16).reshape(prompt_rows, kv_heads * head_width)
    )
    contract = (((1,), (1,)), ((), ()))
    projected = lax.dot_general(
        prompt_keys_grad, key_matrix, contract, preferred_element_type=jnp.float32
    )
    projected = projected + lax.dot_general(
        prompt_values_grad, value_matrix, contract, preferred_element_type=jnp.float32
    )
    prompt_input_grad = lax.psum_scatter(
        projected, "tensor", scatter_dimension=1, tiled=True
    ).astype(jnp.bfloat16)
    resp_share = lax.psum_scatter(resp_terms, "prefix", scatter_dimension=0, tiled=True)
    key_output = resp_share[:, :, 0].astype(jnp.bfloat16)
    value_output = resp_share[:, :, 1].astype(jnp.bfloat16)
    return (query_grad, key_output, value_output, prompt_input_grad)


def solution(mesh):
    placed = (
        P("prefix", "group", "tensor", None),
        P("prefix", "group", "tensor", None),
        P("prefix", "group", "tensor", None),
        P("prefix", "group", "tensor", None),
        P("prefix", "tensor", None),
        P("prefix", "tensor", None),
        P(None, "tensor"),
        P(None, "tensor"),
        P(),
    )
    return jax.shard_map(
        per_device,
        mesh=mesh,
        in_specs=placed,
        out_specs=(
            P("prefix", "group", "tensor", None),
            P("prefix", "group", "tensor", None),
            P("prefix", "group", "tensor", None),
            P("prefix", "tensor"),
        ),
        check_vma=False,
    )
```

profile of v0, /device:TPU:1, one launch (start us, length us, event | category | flops | bytes accessed | tf_op | source)
XLA Modules:
  0.0 260.6 jit_solution(3981751960681253280)
XLA Ops:
  7.3 0.9 dynamic_slice.40
  8.3 2.3 fusion.87
  10.6 1.2 broadcast_select_fusion
  11.8 12.2 %all_gather.12 = bf16[256,2,128]{2,0,1:T(8,128)(2,1)S(1)} all-gather(bf16[64,2,128]{2,0,1:T(8,128)(2,1)S(1)} %copy.66), channel_id=1, replica_groups=mesh['prefix'=4,'group'=4,'tensor'=2] {'prefix'}, dimensions={0}, use_global_device_ids=true | all-gather | bytes 163840 | tf_op jit(solution)/shard_map/all_gather | solution.py:47
  24.0 2.7 %copy.67 = bf16[128,2,16,128]{3,0,2,1:T(8,128)(2,1)} copy(bf16[128,2,16,128]{3,2,1,0:T(8,128)(2,1)} %param.15) | data formatting | bytes 2097152 | tf_op args[0]
  26.7 0.8 bitcast_reduce_fusion
  27.6 0.8 fusion.41
  28.4 1.1 copy-done.5
  29.5 12.6 %all_gather.13 = bf16[512,2,2,128]{3,0,2,1:T(8,128)(2,1)S(1)} all-gather(bf16[128,2,2,128]{3,0,2,1:T(8,128)(2,1)S(1)} %copy.69), channel_id=1, replica_groups=mesh['prefix'=4,'group'=4,'tensor'=2] {'prefix'}, dimensions={0}, use_global_device_ids=true | all-gather | bytes 655360 | tf_op jit(solution)/shard_map/all_gather | solution.py:49
  42.2 14.8 %while.9 = (s32[]{:T(128)}, f32[2,2,8,128]{3,2,1,0:T(8,128)S(1)}, f32[2,2,8,128]{3,2,1,0:T(8,128)S(1)}, s32[4]{0:T(128)S(1)}, bf16[4,128,2,2,128]{4,1,3,2,0:T(8,...) while((s32[]{:T(128)}, f32[2,2,8,128]{3,2,1,0:T(8,128)S(1)}, ...), condition=%wide.region_5.6_spmd.clone, body=%wide.region_2.5_spmd.clone.sunk | while | flops 137912576 | bytes 5638253 | solution.py:76
  43.6 1.7 fusion.115
  47.3 1.7 fusion.115
  51.0 1.7 fusion.115
  54.7 1.7 fusion.115
  57.0 11.2 %all_gather.14 = bf16[256,2,128]{2,0,1:T(8,128)(2,1)S(1)} all-gather(bf16[64,2,128]{2,0,1:T(8,128)(2,1)S(1)} %copy.75), channel_id=1, replica_groups=mesh['prefix'=4,'group'=4,'tensor'=2] {'prefix'}, dimensions={0}, use_global_device_ids=true | all-gather | bytes 163840 | tf_op jit(solution)/shard_map/all_gather | solution.py:48
  68.2 5.8 %fusion.37 = (f32[2,2,8,128]{3,2,0,1:T(8,128)S(1)}, f32[2,128,2,8,256]{1,4,3,2,0:T(8,128)}) fusion(f32[2,256,128,2,8]{2,1,4,3,0:T(8,128)} %copy-done.5, bf16[256,2,128]{2,0,1:T(8,128)(2,1)S(1)} %all_gather.14, bf16[128,2,2,8,128]{4,3,2,1,0:T(8,128)(2,1)} %fusion.87, f32[2,2,8,128]{3,2,1,0:T(8,128)S(1)} %log_add_fusion), kind=kOutput, calls=%fused_computation.58 | convolution fusion | flops 272625664 | bytes 9601024 | tf_op jit(solution)/shard_map/while/body/eval_jaxpr/lrkge,mke->rkglm/dot_general | solution.py:97
  74.0 1.4 copy.74
  75.4 12.7 %all_gather.15 = bf16[512,2,2,128]{3,0,2,1:T(8,128)(2,1)S(1)} all-gather(bf16[128,2,2,128]{3,0,2,1:T(8,128)(2,1)S(1)} %copy.78), channel_id=1, replica_groups=mesh['prefix'=4,'group'=4,'tensor'=2] {'prefix'}, dimensions={0}, use_global_device_ids=true | all-gather | bytes 655360 | tf_op jit(solution)/shard_map/all_gather | solution.py:50
  88.1 0.9 copy.81
  89.0 18.6 %while.10 = (s32[]{:T(128)}, f32[2,2,8,128]{3,2,1,0:T(8,128)S(1)}, s32[4]{0:T(128)S(1)}, bf16[4,128,2,2,128]{4,1,3,2,0:T(8,128)(2,1)S(1)}, bf16[128,2,2,8,128]{4...) while((s32[]{:T(128)}, f32[2,2,8,128]{3,2,1,0:T(8,128)S(1)}, ...), condition=%wide.region_9.10_spmd.clone, body=%wide.region_7.9_spmd.clone.sunk | while | flops 271073536 | bytes 10865305 | solution.py:76
  90.3 1.7 fusion.120
  92.0 1.6 fusion.121
  95.0 1.7 fusion.120
  96.6 1.6 fusion.121
  99.6 1.7 fusion.120
  101.3 1.6 fusion.121
  104.3 1.7 fusion.120
  105.9 1.6 fusion.121
  107.6 5.0 %fusion.43 = (bf16[2,2,8,128,256]{3,4,2,0,1:T(8,128)(2,1)S(1)}, bf16[2,2,8,128,256]{3,4,2,0,1:T(8,128)(2,1)S(1)}) fusion(f32[2,256,128,2,8]{2,1,4,3,0:T(8,128)} %copy-done.5, f32[2,128,2,8,256]{1,4,3,2,0:T(8,128)} %get-tuple-element.414, f32[2,2,8,128]{3,2,1,0:T(8,128)S(1)} %get-tuple-element.659, f32[2,2,8,128]{3,2,1,0:T(8,128)S(1)} %get-tuple-element.701), kind=kLoop, calls=%fused_computation.67 | loop fusion | flops 6291456 | bytes 12615680 | tf_op jit(solution)/shard_map/while/body/eval_jaxpr/convert_element_type | solution.py:114
  112.6 0.7 fusion.51
  113.9 0.7 copy-done.1
  114.6 0.7 fusion.57
  115.3 0.9 pad_maximum_fusion
  116.2 3.9 %convolution_bitcast_fusion.2 = f32[128,2,2,8,128]{4,0,3,1,2:T(8,128)} fusion(bf16[2,2,8,128,256]{3,4,2,0,1:T(8,128)(2,1)} %copy-done.6, bf16[256,2,128]{2,0,1:T(8,128)(2,1)S(1)} %all_gather.12), kind=kOutput, calls=%fused_computation.73 | convolution fusion | flops 268435456 | bytes 4325376 | tf_op jit(solution)/shard_map/while/body/eval_jaxpr/rkglm,mke->lrkge/dot_general | solution.py:122
  120.1 2.9 %copy.84 = f32[128,2,2,8,128]{0,4,3,2,1:T(8,128)} copy(f32[128,2,2,8,128]{4,0,3,1,2:T(8,128)} %convolution_bitcast_fusion.2) | data formatting | bytes 4194304
  123.0 24.1 %reduce-scatter.7.cloned.1.call-done = f32[64,2,2,128]{3,0,2,1:T(8,128)} async-done(((f32[256,2,2,128]{3,0,2,1:T(8,128)}), f32[64,2,2,128]{3,0,2,1:T(8,128)}) %reduce-scatter.7.cloned.1.call-update) | async-done | bytes 131088 | tf_op jit(solution)/shard_map/reduce_scatter | solution.py:137
  147.1 14.4 %all-reduce.1 = bf16[64,2,2,128]{3,0,2,1:T(8,128)(2,1)S(1)} all-reduce(f32[64,2,2,128]{3,0,2,1:T(8,128)} %reduce-scatter.7.cloned.1.call-done), channel_id=1, replica_groups=mesh['prefix'=4,'group'=4,'tensor'=2] {'group'}, use_global_device_ids=true, to_apply=%region_14.15 | all-reduce | flops 32768 | bytes 196608 | tf_op jit(solution)/shard_map/psum | solution.py:138
  161.6 0.9 fusion.70
  162.5 0.7 copy-done.11
  163.2 2.0 convolution_add_fusion
  165.3 40.7 %while.11 = (s32[]{:T(128)}, f32[128,2,2,8,128]{0,4,3,2,1:T(8,128)}, f32[4,128,2,2,2,128]{5,4,2,3,1,0:T(2,128)}, bf16[4,128,2,2,128]{4,1,3,2,0:T(8,128)(2,1)S(1)...) while((s32[]{:T(128)}, ...), condition=%wide.region_11.12_spmd.clone, body=%wide.region_10.11_spmd.clone.sunk | while | flops 675496192 | bytes 29297864 | solution.py:76
  166.6 1.8 fusion.132
  168.5 1.4 fusion.133
  170.8 1.2 copy_dynamic-update-slice_fusion.2
  172.0 3.4 %bitcast_add_fusion.2 = f32[128,2,2,8,128]{0,4,3,2,1:T(8,128)} fusion(f32[128,2,2,8,128]{0,4,3,2,1:T(8,128)} %get-tuple-element.663, bf16[2,2,8,128,128]{3,4,2,1,0:T(8,128)(2,1)S(1)} %fusion.133, bf16[4,128,2,2,128]{4,1,3,2,0:T(8,128)(2,1)S(1)} %get-tuple-element.677, s32[]{:T(128)} %get-tuple-element.662), kind=kOutput, calls=%fused_computation.29.clone.1 | convolution fusion | flops 134742016 | bytes 5373956 | tf_op jit(solution)/shard_map/while/body/eval_jaxpr/rkglm,mrke->lrkge/dot_general | solution.py:122
  176.8 1.8 fusion.132
  178.6 1.4 fusion.133
  181.0 1.2 copy_dynamic-update-slice_fusion.2
  182.2 3.5 %bitcast_add_fusion.2 = f32[128,2,2,8,128]{0,4,3,2,1:T(8,128)} fusion(f32[128,2,2,8,128]{0,4,3,2,1:T(8,128)} %get-tuple-element.663, bf16[2,2,8,128,128]{3,4,2,1,0:T(8,128)(2,1)S(1)} %fusion.133, bf16[4,128,2,2,128]{4,1,3,2,0:T(8,128)(2,1)S(1)} %get-tuple-element.677, s32[]{:T(128)} %get-tuple-element.662), kind=kOutput, calls=%fused_computation.29.clone.1 | convolution fusion | flops 134742016 | bytes 5373956 | tf_op jit(solution)/shard_map/while/body/eval_jaxpr/rkglm,mrke->lrkge/dot_general | solution.py:122
  187.0 1.8 fusion.132
  188.8 1.4 fusion.133
  191.2 1.2 copy_dynamic-update-slice_fusion.2
  192.4 3.4 %bitcast_add_fusion.2 = f32[128,2,2,8,128]{0,4,3,2,1:T(8,128)} fusion(f32[128,2,2,8,128]{0,4,3,2,1:T(8,128)} %get-tuple-element.663, bf16[2,2,8,128,128]{3,4,2,1,0:T(8,128)(2,1)S(1)} %fusion.133, bf16[4,128,2,2,128]{4,1,3,2,0:T(8,128)(2,1)S(1)} %get-tuple-element.677, s32[]{:T(128)} %get-tuple-element.662), kind=kOutput, calls=%fused_computation.29.clone.1 | convolution fusion | flops 134742016 | bytes 5373956 | tf_op jit(solution)/shard_map/while/body/eval_jaxpr/rkglm,mrke->lrkge/dot_general | solution.py:122
  197.2 1.8 fusion.132
  199.0 1.4 fusion.133
  201.4 1.2 copy_dynamic-update-slice_fusion.2
  202.6 3.4 %bitcast_add_fusion.2 = f32[128,2,2,8,128]{0,4,3,2,1:T(8,128)} fusion(f32[128,2,2,8,128]{0,4,3,2,1:T(8,128)} %get-tuple-element.663, bf16[2,2,8,128,128]{3,4,2,1,0:T(8,128)(2,1)S(1)} %fusion.133, bf16[4,128,2,2,128]{4,1,3,2,0:T(8,128)(2,1)S(1)} %get-tuple-element.677, s32[]{:T(128)} %get-tuple-element.662), kind=kOutput, calls=%fused_computation.29.clone.1 | convolution fusion | flops 134742016 | bytes 5373956 | tf_op jit(solution)/shard_map/while/body/eval_jaxpr/rkglm,mrke->lrkge/dot_general | solution.py:122
  206.0 3.9 %reshape.120 = f32[512,1024]{1,0:T(8,128)} reshape(f32[512,2,2,2,128]{4,3,2,1,0:T(2,128)} %bitcast.266) | data formatting | bytes 4194304
  210.0 2.9 %multiply_convert_fusion = bf16[128,2,2,8,128]{0,4,3,2,1:T(8,128)(2,1)} fusion(f32[128,2,2,8,128]{0,4,3,2,1:T(8,128)} %get-tuple-element.213), kind=kLoop, calls=%fused_computation.72 | loop fusion | flops 1048576 | bytes 3145728 | tf_op jit(solution)/shard_map/convert_element_type | solution.py:134
  212.8 2.6 %copy.87 = bf16[128,2,2,8,128]{4,3,2,1,0:T(8,128)(2,1)} copy(bf16[128,2,2,8,128]{0,4,3,2,1:T(8,128)(2,1)} %multiply_convert_fusion) | data formatting | bytes 2097152 | tf_op jit(solution)/shard_map/convert_element_type | solution.py:134
  215.5 1.8 convert_element_type.45
  217.3 34.7 %reduce-scatter.11.cloned.1.call-done = f32[128,1024]{1,0:T(8,128)} async-done(((f32[512,1024]{1,0:T(8,128)}), f32[128,1024]{1,0:T(8,128)}) %reduce-scatter.11.cloned.1.call-update) | async-done | bytes 524304
  252.0 1.1 reshape.121
  253.2 0.9 slice_bitcast_fusion
  (140 shorter events, 23.0 us)
Async XLA Ops:
  7.2 154.4 %copy-start = (bf16[5120,256]{1,0:T(8,128)(2,1)S(1)}, bf16[5120,256]{1,0:T(8,128)(2,1)}, u32[]{:S(2)}) copy-start(bf16[5120,256]{1,0:T(8,128)(2,1)} %param.21) | copy-start | bytes 7864324
  7.2 139.9 %reduce-scatter.7.cloned.1.call-start = ((), (), s32[]{:S(2)}) async-start(), calls=%async_computation.3 | async-start | bytes 655360 | tf_op jit(solution)/shard_map/reduce_scatter | solution.py:137
  7.3 3.3 %copy-start.8 = (bf16[128,2,16,128]{3,2,1,0:T(8,128)(2,1)S(1)}, bf16[128,2,16,128]{3,2,1,0:T(8,128)(2,1)}, u32[]{:S(2)}) copy-start(bf16[128,2,16,128]{3,2,1,0:T(8,128)(2,1)} %param.18) | copy-start | bytes 3145732
  8.3 3.5 %copy-start.14 = (bf16[64,2,128]{2,1,0:T(2,128)(2,1)S(1)}, bf16[64,2,128]{2,1,0:T(2,128)(2,1)}, u32[]{:S(2)}) copy-start(bf16[64,2,128]{2,1,0:T(2,128)(2,1)} %param.19) | copy-start | bytes 98308
  11.8 14.9 %copy-start.10 = (bf16[128,2,16,128]{3,2,1,0:T(8,128)(2,1)S(1)}, bf16[128,2,16,128]{3,2,1,0:T(8,128)(2,1)}, u32[]{:S(2)}) copy-start(bf16[128,2,16,128]{3,2,1,0:T(8,128)(2,1)} %param.15) | copy-start | bytes 3145732
  27.5 1.9 copy-start.5
  27.6 1.9 copy-start.12
  42.2 14.8 %copy-start.15 = (bf16[64,2,128]{2,1,0:T(2,128)(2,1)S(1)}, bf16[64,2,128]{2,1,0:T(2,128)(2,1)}, u32[]{:S(2)}) copy-start(bf16[64,2,128]{2,1,0:T(2,128)(2,1)} %param.20) | copy-start | bytes 98308
  68.2 5.8 %copy-start.9 = (bf16[128,2,16,128]{3,2,1,0:T(8,128)(2,1)S(1)}, bf16[128,2,16,128]{3,2,1,0:T(8,128)(2,1)}, u32[]{:S(2)}) copy-start(bf16[128,2,16,128]{3,2,1,0:T(8,128)(2,1)} %broadcast_select_fusion) | copy-start | bytes 3145732
  74.0 1.4 copy-start.13
  89.0 3.0 %copy-start.3 = (bf16[128,2,2,8,128]{4,0,3,2,1:T(8,128)(2,1)S(1)}, bf16[128,2,2,8,128]{4,0,3,2,1:T(8,128)(2,1)}, u32[]{:S(2)}) copy-start(bf16[128,2,2,8,128]{4,0,3,2,1:T(8,128)(2,1)} %get-tuple-element.647) | copy-start | bytes 3145732 | tf_op jit(solution)/shard_map/while
  93.6 3.0 %copy-start.3 = (bf16[128,2,2,8,128]{4,0,3,2,1:T(8,128)(2,1)S(1)}, bf16[128,2,2,8,128]{4,0,3,2,1:T(8,128)(2,1)}, u32[]{:S(2)}) copy-start(bf16[128,2,2,8,128]{4,0,3,2,1:T(8,128)(2,1)} %get-tuple-element.647) | copy-start | bytes 3145732 | tf_op jit(solution)/shard_map/while
  98.3 3.0 %copy-start.3 = (bf16[128,2,2,8,128]{4,0,3,2,1:T(8,128)(2,1)S(1)}, bf16[128,2,2,8,128]{4,0,3,2,1:T(8,128)(2,1)}, u32[]{:S(2)}) copy-start(bf16[128,2,2,8,128]{4,0,3,2,1:T(8,128)(2,1)} %get-tuple-element.647) | copy-start | bytes 3145732 | tf_op jit(solution)/shard_map/while
  102.9 3.0 %copy-start.3 = (bf16[128,2,2,8,128]{4,0,3,2,1:T(8,128)(2,1)S(1)}, bf16[128,2,2,8,128]{4,0,3,2,1:T(8,128)(2,1)}, u32[]{:S(2)}) copy-start(bf16[128,2,2,8,128]{4,0,3,2,1:T(8,128)(2,1)} %get-tuple-element.647) | copy-start | bytes 3145732 | tf_op jit(solution)/shard_map/while
  107.6 5.0 %copy-start.7 = (bf16[128,2,2,8,128]{4,3,2,1,0:T(8,128)(2,1)S(1)}, bf16[128,2,2,8,128]{4,3,2,1,0:T(8,128)(2,1)}, u32[]{:S(2)}) copy-start(bf16[128,2,2,8,128]{4,3,2,1,0:T(8,128)(2,1)} %fusion.87) | copy-start | bytes 3145732
  112.6 1.3 copy-start.6
  112.6 2.0 copy-start.1
  116.2 99.3 %reduce-scatter.9.cloned.1.call-start = ((), (), s32[]{:S(2)}) async-start(), calls=%async_computation.4 | async-start | bytes 1966080 | tf_op jit(solution)/shard_map/reduce_scatter | solution.py:152
  161.5 1.7 copy-start.11
  165.2 86.8 %reduce-scatter.11.cloned.1.call-start = ((), (), s32[]{:S(2)}) async-start(), calls=%async_computation.5 | async-start | bytes 2621440
  165.3 3.2 %copy-start.4 = (bf16[128,2,2,8,128]{4,0,3,2,1:T(8,128)(2,1)S(1)}, bf16[128,2,2,8,128]{4,0,3,2,1:T(8,128)(2,1)}, u32[]{:S(2)}) copy-start(bf16[128,2,2,8,128]{4,0,3,2,1:T(8,128)(2,1)} %get-tuple-element.682) | copy-start | bytes 3145732 | tf_op jit(solution)/shard_map/while
  168.5 1.5 copy-start.2
  175.5 3.2 %copy-start.4 = (bf16[128,2,2,8,128]{4,0,3,2,1:T(8,128)(2,1)S(1)}, bf16[128,2,2,8,128]{4,0,3,2,1:T(8,128)(2,1)}, u32[]{:S(2)}) copy-start(bf16[128,2,2,8,128]{4,0,3,2,1:T(8,128)(2,1)} %get-tuple-element.682) | copy-start | bytes 3145732 | tf_op jit(solution)/shard_map/while
  178.6 1.5 copy-start.2
  185.7 3.2 %copy-start.4 = (bf16[128,2,2,8,128]{4,0,3,2,1:T(8,128)(2,1)S(1)}, bf16[128,2,2,8,128]{4,0,3,2,1:T(8,128)(2,1)}, u32[]{:S(2)}) copy-start(bf16[128,2,2,8,128]{4,0,3,2,1:T(8,128)(2,1)} %get-tuple-element.682) | copy-start | bytes 3145732 | tf_op jit(solution)/shard_map/while
  188.8 1.5 copy-start.2
  195.8 3.2 %copy-start.4 = (bf16[128,2,2,8,128]{4,0,3,2,1:T(8,128)(2,1)S(1)}, bf16[128,2,2,8,128]{4,0,3,2,1:T(8,128)(2,1)}, u32[]{:S(2)}) copy-start(bf16[128,2,2,8,128]{4,0,3,2,1:T(8,128)(2,1)} %get-tuple-element.682) | copy-start | bytes 3145732 | tf_op jit(solution)/shard_map/while
  199.0 1.5 copy-start.2
Sparse Core Ops, SparseCore 0:
  116.3 30.7 reduce-scatter.6
  165.3 21.4 reduce-scatter.8
  210.1 41.9 reduce-scatter.10
where the time goes:
time: 263 us; the launch traced here: 261 us
  matrix products  64.7 us (25%)
  blocking collectives  63.2 us (24%)
  waiting for transfers between devices  58.9 us (22%)
  local copies, waits for them, and re-layouts  32.8 us (12%)
  other arithmetic  26.1 us (10%)
  between operations  14.1 us (5%)
    unnamed x4, waiting for transfers between devices  34.8 us
    reduce_scatter x1, waiting for transfers between devices, per_device(): lax.psum_scatter(prompt_terms, 'prefix', scatter_dimension=0, tiled=True)  24.1 us
    dot_general x13, matrix products, score_block(): jnp.einsum(einsum_forms[0], queries, key_block, preferred_element_type=jn...  21.5 us
    dot_general x9, matrix products, prob_block(): jnp.einsum(einsum_forms[0], cotangent, value_block, preferred_element_typ...  17.9 us
    dot_general x5, matrix products, grad_step(): jnp.einsum(einsum_forms[2], attn_dscore, key_block, preferred_element_typ...  17.6 us
    unnamed x39, local copies, waits for them, and re-layouts  14.7 us
    psum x1, blocking collectives, per_device(): prompt_share = lax.psum(prompt_share, 'group')  14.4 us
    all_gather x1, blocking collectives, per_device(): lax.all_gather(response_value, 'prefix', axis=0, tiled=True)  12.7 us
  transfers between devices with their start and end apart: 3, of which 2 were waited for; matrix products, arithmetic and copies ran while one was open for 22% of the time, Pallas kernels for 0%

commit v1 on v0

v1 whole, which is shorter than its diff:
```python
import functools
import math

import jax
import jax.numpy as jnp
from jax import lax
from jax.experimental import pallas as pl
from jax.experimental.pallas import tpu as pltpu
from jax.sharding import PartitionSpec as P

MESH = pl.DeviceIdType.MESH
masked_score = -1e30
log2_e = math.log2(math.e)


def dot_nt(a, b):
    return lax.dot_general(a, b, (((1,), (1,)), ((), ())), preferred_element_type=jnp.float32)


def dot_nn(a, b):
    return lax.dot_general(a, b, (((1,), (0,)), ((), ())), preferred_element_type=jnp.float32)


def kernel(
    sizes,
    len_ref,
    kv_ref,
    pr_ref,
    q_ref,
    cot_ref,
    km_ref,
    vm_ref,
    dq_ref,
    dkv_ref,
    out_ref,
    qs,
    cots,
    kv_all,
    pr_all,
    m_ref,
    l_ref,
    d_ref,
    dq_acc,
    own,
    gsend,
    grecv,
    pacc,
    ps1,
    pr1,
    ps2,
    pr2,
    pg_all,
    weights,
    opart,
    xs,
    xr,
    og,
    w_sem,
    c_send,
    c_recv,
    a_send,
    a_recv,
    b_send,
    b_recv,
    g_send,
    g_recv,
    r1_send,
    r1_recv,
    r2_send,
    r2_recv,
    r3_send,
    r3_recv,
    x_send,
    x_recv,
    o_send,
    o_recv,
):
    n, G, T = sizes
    p = lax.axis_index("prefix")
    g = lax.axis_index("group")
    t = lax.axis_index("tensor")
    L, R, heads, E = q_ref.shape
    pairs = kv_ref.shape[0]
    H = pairs // R
    F = heads // H
    rows = L * F
    piece = pr_ref.shape[3]
    quarter = weights.shape[2]
    scale = 1.0 / math.sqrt(E)
    log_scale = scale * log2_e

    def at(pp=None, gg=None, tt=None):
        return (p if pp is None else pp, g if gg is None else gg, t if tt is None else tt)

    def peer(me, o, size):
        return lax.rem(me + o, size)

    def remote(src, dst, send, recv, where):
        return pltpu.make_async_remote_copy(
            src_ref=src, dst_ref=dst, send_sem=send, recv_sem=recv, device_id=where, device_id_type=MESH
        )

    barrier = pltpu.get_barrier_semaphore()
    for o in range(1, n):
        pl.semaphore_signal(barrier, inc=1, device_id=at(pp=peer(p, o, n)), device_id_type=MESH)
    for o in range(1, G):
        pl.semaphore_signal(barrier, inc=1, device_id=at(gg=peer(g, o, G)), device_id_type=MESH)
    for o in range(1, T):
        pl.semaphore_signal(barrier, inc=1, device_id=at(tt=peer(t, o, T)), device_id_type=MESH)

    half = quarter * G

    def weight_copies():
        copies = []
        for which, ref in enumerate((km_ref, vm_ref)):
            for tt in range(T):
                start = pl.multiple_of(tt * half + g * quarter, 16)
                copies.append(
                    pltpu.make_async_copy(
                        ref.at[pl.ds(start, quarter)], weights.at[which, tt], w_sem.at[which, tt]
                    )
                )
        return copies

    for copy in weight_copies():
        copy.start()

    pl.semaphore_wait(barrier, n + G + T - 3)

    def chunk_copy(src, j):
        return remote(src, kv_all.at[j], c_send.at[j], c_recv.at[j], at(pp=lax.rem(p + 1, n)))

    @pl.when(p < n - 1)
    def _():
        chunk_copy(kv_ref, p).start()

    def prompt_a(o):
        dest = peer(p, o, n)
        return remote(pr_ref.at[g], pr_all.at[p, g], a_send.at[dest], a_recv.at[p], at(pp=dest))

    def prompt_a_wait(o):
        src = peer(p, o, n)
        remote(pr_ref.at[g], pr_all.at[src, g], a_send.at[src], a_recv.at[src], at(pp=src)).wait_recv()

    for o in range(1, n):
        prompt_a(o).start()

    pos = p * L + lax.broadcasted_iota(jnp.int32, (L, F, E), 0)
    for r in range(R):
        length = len_ref[g * R + r]
        q = q_ref[:, r].astype(jnp.float32)
        c = cot_ref[:, r].astype(jnp.float32)
        for h in range(H):
            qs[r * H + h] = q[:, h * F : (h + 1) * F].reshape(rows, E).astype(jnp.bfloat16)
            live = jnp.where(pos < length, c[:, h * F : (h + 1) * F], 0.0)
            cots[r * H + h] = live.reshape(rows, E).astype(jnp.bfloat16)
    pr_all[p] = pr_ref[...]

    def scores(pair, k, diag):
        s = dot_nt(k, qs[pair]) * log_scale
        if diag:
            key = lax.broadcasted_iota(jnp.int32, s.shape, 0)
            query = lax.broadcasted_iota(jnp.int32, s.shape, 1) // F
            s = jnp.where(key <= query, s, masked_score)
        return s

    def stats(pair, k, v, diag):
        s = scores(pair, k, diag)
        dp = dot_nt(v, cots[pair])
        if diag:
            m_new = jnp.max(s, axis=0, keepdims=True)
            e = jnp.exp2(s - m_new)
            l_ref[pair] = jnp.sum(e, axis=0, keepdims=True)
            d_ref[pair] = jnp.sum(e * dp, axis=0, keepdims=True)
        else:
            m_old = m_ref[pair]
            m_new = jnp.maximum(m_old, jnp.max(s, axis=0, keepdims=True))
            e = jnp.exp2(s - m_new)
            a = jnp.exp2(m_old - m_new)
            l_ref[pair] = l_ref[pair] * a + jnp.sum(e, axis=0, keepdims=True)
            d_ref[pair] = d_ref[pair] * a + jnp.sum(e * dp, axis=0, keepdims=True)
        m_ref[pair] = m_new

    def each_pair(body):
        def step(i, carry):
            body(i)
            return carry

        lax.fori_loop(0, pairs, step, 0)

    def prompt_block(which, pair):
        return pr_all[:, :, which, lax.rem(pair, H)].reshape(n * G * piece, E)

    each_pair(lambda i: stats(i, kv_ref[i, 0], kv_ref[i, 1], True))

    def prompt_b(o, oo):
        src, dest = peer(p, o, n), peer(g, oo, G)
        return remote(
            pr_all.at[src, g], pr_all.at[src, g], b_send.at[dest, src], b_recv.at[g, src], at(gg=dest)
        )

    def prompt_b_wait(o, oo):
        src, frm = peer(p, o, n), peer(g, oo, G)
        remote(
            pr_all.at[src, frm], pr_all.at[src, frm], b_send.at[frm, src], b_recv.at[frm, src], at(gg=frm)
        ).wait_recv()

    for o in range(1, n):
        prompt_a_wait(o)
        for oo in range(1, G):
            prompt_b(o, oo).start()

    def prompt_stats():
        for o in range(1, n):
            for oo in range(1, G):
                prompt_b_wait(o, oo)
        each_pair(lambda i: stats(i, prompt_block(0, i), prompt_block(1, i), False))

    def chunk_step(s, carry):
        j = p - s
        chunk_copy(kv_ref, j).wait_recv()

        @pl.when(p < n - 1)
        def _():
            chunk_copy(kv_all.at[j], j).start()

        each_pair(lambda i: stats(i, kv_all[j, i, 0], kv_all[j, i, 1], False))
        return carry

    lax.fori_loop(1, jnp.minimum(p, 1) + 1, chunk_step, 0)
    prompt_stats()
    lax.fori_loop(2, p + 1, chunk_step, 0)

    def finish(i):
        d_ref[i] = d_ref[i] / l_ref[i]
        m_ref[i] = m_ref[i] + jnp.log(l_ref[i]) * log2_e
        dq_acc[i] = jnp.zeros((E, rows), jnp.float32)

    each_pair(finish)

    def grads(pair, k, v, diag):
        prob = jnp.exp2(scores(pair, k, diag) - m_ref[pair])
        dp = dot_nt(v, cots[pair])
        ds = (prob * (dp - d_ref[pair])).astype(jnp.bfloat16)
        dv = dot_nn(prob.astype(jnp.bfloat16), cots[pair])
        dk = dot_nn(ds, qs[pair]) * scale
        dq_acc[pair] += dot_nn(k.T, ds)
        return dk, dv

    def grad_copy(j, i):
        return remote(
            gsend.at[j, i], grecv.at[j, i], g_send.at[j, i], g_recv.at[j, i], at(pp=lax.rem(p + n - 1, n))
        )

    def chunk_grads(j, carry):
        def body(i):
            dk, dv = grads(i, kv_all[j, i, 0], kv_all[j, i, 1], False)

            @pl.when(p == n - 1)
            def _():
                gsend[j, i, 0] = dk.astype(jnp.bfloat16)
                gsend[j, i, 1] = dv.astype(jnp.bfloat16)
                grad_copy(j, i).start()

            @pl.when(p < n - 1)
            def _():
                own[j, i, 0] = dk
                own[j, i, 1] = dv

        each_pair(body)
        return carry

    lax.fori_loop(0, jnp.minimum(p, 1), chunk_grads, 0)

    pacc[...] = jnp.zeros_like(pacc)

    def prompt_grads(i):
        dk, dv = grads(i, prompt_block(0, i), prompt_block(1, i), False)
        h = lax.rem(i, H)
        dk = dk.reshape(n, G, piece, E)
        dv = dv.reshape(n, G, piece, E)
        for gg in range(G):
            pacc[gg, :, 0, h] += dk[:, gg]
            pacc[gg, :, 1, h] += dv[:, gg]

    each_pair(prompt_grads)
    ps1[...] = pacc[...].astype(jnp.bfloat16)

    def r1(o):
        dest = peer(g, o, G)
        return remote(ps1.at[dest], pr1.at[g], r1_send.at[dest], r1_recv.at[g], at(gg=dest))

    def r1_wait(o):
        src = peer(g, o, G)
        remote(ps1.at[src], pr1.at[src], r1_send.at[src], r1_recv.at[src], at(gg=src)).wait_recv()

    for o in range(1, G):
        r1(o).start()

    lax.fori_loop(1, p, chunk_grads, 0)

    def own_grads(i):
        dk, dv = grads(i, kv_ref[i, 0], kv_ref[i, 1], True)

        @pl.when(p == n - 1)
        def _():
            dkv_ref[i, 0] = dk.astype(jnp.bfloat16)
            dkv_ref[i, 1] = dv.astype(jnp.bfloat16)

        @pl.when(p < n - 1)
        def _():
            own[p, i, 0] = dk
            own[p, i, 1] = dv

    each_pair(own_grads)

    for o in range(1, G):
        r1_wait(o)
    pacc[g] = functools.reduce(
        lambda a, b: a + b, [pr1[peer(g, o, G)].astype(jnp.float32) for o in range(1, G)], pacc[g]
    )
    ps2[...] = pacc[g].astype(jnp.bfloat16)

    def r2(o):
        dest = peer(p, o, n)
        return remote(ps2.at[dest], pr2.at[p], r2_send.at[dest], r2_recv.at[p], at(pp=dest))

    def r2_wait(o):
        src = peer(p, o, n)
        remote(ps2.at[src], pr2.at[src], r2_send.at[src], r2_recv.at[src], at(pp=src)).wait_recv()

    for o in range(1, n):
        r2(o).start()

    for r in range(R):
        parts = [dq_acc[r * H + h].T.reshape(L, F, E) for h in range(H)]
        dq_ref[:, r] = (jnp.concatenate(parts, axis=1) * scale).astype(jnp.bfloat16)

    def relay(slot):
        j = slot - (n - 1 - p)

        @pl.when((p < n - 1) & (j >= 0))
        def _():
            def body(i):
                grad_copy(j, i).wait_recv()
                total = own[j, i] + grecv[j, i].astype(jnp.float32)
                low = total.astype(jnp.bfloat16)

                @pl.when(j < p)
                def _():
                    gsend[j, i] = low
                    grad_copy(j, i).start()

                @pl.when(j == p)
                def _():
                    dkv_ref[i] = low

            each_pair(body)

    for slot in range(1, n - 2):
        relay(slot)

    for o in range(1, n):
        r2_wait(o)
    total = pacc[g, p]
    for o in range(1, n):
        total = total + pr2[peer(p, o, n)].astype(jnp.float32)
    pg_all[g] = total.astype(jnp.bfloat16)

    def r3(o):
        dest = peer(g, o, G)
        return remote(pg_all.at[g], pg_all.at[g], r3_send.at[dest], r3_recv.at[g], at(gg=dest))

    def r3_wait(o):
        src = peer(g, o, G)
        remote(pg_all.at[src], pg_all.at[src], r3_send.at[src], r3_recv.at[src], at(gg=src)).wait_recv()

    for o in range(1, G):
        r3(o).start()
    for copy in weight_copies():
        copy.wait()
    for o in range(1, G):
        r3_wait(o)

    def project(tt):
        result = None
        for which in range(2):
            for h in range(H):
                low = pg_all[:, which, h].reshape(G * piece, E)
                term = dot_nt(low, weights[which, tt, :, h * E : (h + 1) * E])
                result = term if result is None else result + term
        return result

    def x_copy(o):
        dest = peer(t, o, T)
        return remote(xs.at[o - 1], xr.at[o - 1], x_send.at[o - 1], x_recv.at[o - 1], at(tt=dest))

    for o in range(1, T):
        xs[o - 1] = project(peer(t, o, T)).astype(jnp.bfloat16)
        x_copy(o).start()
    opart[...] = project(t)

    if n > 2:
        relay(n - 2)

    result = opart[...]
    for o in range(1, T):
        x_copy(o).wait_recv()
        result = result + xr[o - 1].astype(jnp.float32)
    og[g] = result.astype(jnp.bfloat16)

    def o_copy(o):
        dest = peer(g, o, G)
        return remote(og.at[g], og.at[g], o_send.at[dest], o_recv.at[g], at(gg=dest))

    def o_wait(o):
        src = peer(g, o, G)
        remote(og.at[src], og.at[src], o_send.at[src], o_recv.at[src], at(gg=src)).wait_recv()

    for o in range(1, G):
        o_copy(o).start()
    relay(n - 1)
    for o in range(1, G):
        o_wait(o)
    for gg in range(G):
        out_ref[:, gg * quarter : (gg + 1) * quarter] = og[gg]

    def chunk_sent(j, carry):
        chunk_copy(kv_ref, j).wait_send()
        return carry

    @pl.when(p < n - 1)
    def _():
        lax.fori_loop(0, p + 1, chunk_sent, 0)

    def grads_sent(j, carry):
        each_pair(lambda i: grad_copy(j, i).wait_send())
        return carry

    lax.fori_loop(0, p, grads_sent, 0)
    for o in range(1, n):
        prompt_a(o).wait_send()
        r2(o).wait_send()
        for oo in range(1, G):
            prompt_b(o, oo).wait_send()
    for o in range(1, G):
        r1(o).wait_send()
        r3(o).wait_send()
        o_copy(o).wait_send()
    for o in range(1, T):
        x_copy(o).wait_send()


def per_device(
    sizes,
    resp_query,
    response_key,
    response_value,
    resp_cotangent,
    prompt_key,
    prompt_value_rows,
    key_matrix,
    value_matrix,
    resp_lengths,
):
    n, G, T = sizes
    L, R, heads, E = resp_query.shape
    H = response_key.shape[2]
    pairs = R * H
    rows = L * heads // H
    prompt_rows = prompt_key.shape[0]
    piece = prompt_rows // G
    width = key_matrix.shape[0]
    quarter = width // T // G
    bf16, f32 = jnp.bfloat16, jnp.float32

    kv = jnp.stack((response_key, response_value), axis=0)
    kv = kv.transpose(2, 3, 0, 1, 4).reshape(pairs, 2, L, E)
    prompt = jnp.stack((prompt_key, prompt_value_rows), axis=0)
    prompt = prompt.reshape(2, G, piece, H, E).transpose(1, 0, 3, 2, 4)

    vmem = pl.BlockSpec(memory_space=pltpu.VMEM)
    dma = pltpu.SemaphoreType.DMA
    scratch = [
        pltpu.VMEM((pairs, rows, E), bf16),
        pltpu.VMEM((pairs, rows, E), bf16),
        pltpu.VMEM((n, pairs, 2, L, E), bf16),
        pltpu.VMEM((n, G, 2, H, piece, E), bf16),
        pltpu.VMEM((pairs, 1, rows), f32),
        pltpu.VMEM((pairs, 1, rows), f32),
        pltpu.VMEM((pairs, 1, rows), f32),
        pltpu.VMEM((pairs, E, rows), f32),
        pltpu.VMEM((n, pairs, 2, L, E), f32),
        pltpu.VMEM((n, pairs, 2, L, E), bf16),
        pltpu.VMEM((n, pairs, 2, L, E), bf16),
        pltpu.VMEM((G, n, 2, H, piece, E), f32),
        pltpu.VMEM((G, n, 2, H, piece, E), bf16),
        pltpu.VMEM((G, n, 2, H, piece, E), bf16),
        pltpu.VMEM((n, 2, H, piece, E), bf16),
        pltpu.VMEM((n, 2, H, piece, E), bf16),
        pltpu.VMEM((G, 2, H, piece, E), bf16),
        pltpu.VMEM((2, T, quarter, H * E), bf16),
        pltpu.VMEM((prompt_rows, quarter), f32),
        pltpu.VMEM((max(T - 1, 1), prompt_rows, quarter), bf16),
        pltpu.VMEM((max(T - 1, 1), prompt_rows, quarter), bf16),
        pltpu.VMEM((G, prompt_rows, quarter), bf16),
        dma((2, T)),
        dma((n,)),
        dma((n,)),
        dma((n,)),
        dma((n,)),
        dma((G, n)),
        dma((G, n)),
        dma((n, pairs)),
        dma((n, pairs)),
        dma((G,)),
        dma((G,)),
        dma((n,)),
        dma((n,)),
        dma((G,)),
        dma((G,)),
        dma((max(T - 1, 1),)),
        dma((max(T - 1, 1),)),
        dma((G,)),
        dma((G,)),
    ]
    query_grad, kv_grad, out = pl.pallas_call(
        functools.partial(kernel, sizes),
        out_shape=(
            jax.ShapeDtypeStruct((L, R, heads, E), bf16),
            jax.ShapeDtypeStruct((pairs, 2, L, E), bf16),
            jax.ShapeDtypeStruct((prompt_rows, width // T), bf16),
        ),
        in_specs=[
            pl.BlockSpec(memory_space=pltpu.SMEM),
            vmem,
            vmem,
            vmem,
            vmem,
            pl.BlockSpec(memory_space=pl.ANY),
            pl.BlockSpec(memory_space=pl.ANY),
        ],
        out_specs=(vmem, vmem, vmem),
        scratch_shapes=scratch,
        compiler_params=pltpu.CompilerParams(
            collective_id=0, has_side_effects=True, vmem_limit_bytes=60 * 1024 * 1024
        ),
    )(resp_lengths, kv, prompt, resp_query, resp_cotangent, key_matrix, value_matrix)
    kv_grad = kv_grad.reshape(R, H, 2, L, E).transpose(2, 3, 0, 1, 4)
    return (query_grad, kv_grad[0], kv_grad[1], out)


def solution(mesh):
    sizes = (mesh.shape["prefix"], mesh.shape["group"], mesh.shape["tensor"])
    placed = (
        P("prefix", "group", "tensor", None),
        P("prefix", "group", "tensor", None),
        P("prefix", "group", "tensor", None),
        P("prefix", "group", "tensor", None),
        P("prefix", "tensor", None),
        P("prefix", "tensor", None),
        P(None, "tensor"),
        P(None, "tensor"),
        P(),
    )
    return jax.shard_map(
        functools.partial(per_device, sizes),
        mesh=mesh,
        in_specs=placed,
        out_specs=(
            P("prefix", "group", "tensor", None),
            P("prefix", "group", "tensor", None),
            P("prefix", "group", "tensor", None),
            P("prefix", "tensor"),
        ),
        check_vma=False,
    )
```

time: 263 us -> 75.9 us (0.29)
  Pallas kernels: 0 us -> 65.4 us
  matrix products: 64.7 us -> 0 us
  blocking collectives: 63.2 us -> 0 us
  waiting for transfers between devices: 58.9 us -> 0 us
  local copies, waits for them, and re-layouts: 32.8 us -> 7.46 us
  other arithmetic: 26.1 us -> 1.99 us
  between operations: 14.1 us -> 0.66 us
    pallas_call x0 -> x1, Pallas kernels: none -> 65.4 us  [per_device(): pl.pallas_call(functools.partial(kernel, sizes), out_shape=(jax.ShapeDtyp...]
    dot_general x39 -> x0, matrix products: 64.7 us -> none  [the longest x13 21.5 us: score_block(): jnp.einsum(einsum_forms[0], queries, key_block, preferred_element_type=jn...]
    all_gather x4 -> x0, blocking collectives: 48.8 us -> none  [the longest x1 12.7 us: per_device(): lax.all_gather(response_value, 'prefix', axis=0, tiled=True)]
    unnamed x4 -> x0, waiting for transfers between devices: 34.8 us -> none
    reduce_scatter x2 -> x0, waiting for transfers between devices: 24.1 us -> none  [the longest x1 24.1 us: per_device(): lax.psum_scatter(prompt_terms, 'prefix', scatter_dimension=0, tiled=True)]
    psum x1 -> x0, blocking collectives: 14.4 us -> none  [per_device(): prompt_share = lax.psum(prompt_share, 'group')]
    unnamed x39 -> x4, local copies, waits for them, and re-layouts: 14.7 us -> 3.05 us
    convert_element_type x3 -> x0, other arithmetic: 9.7 us -> none  [the longest x1 4.99 us: grad_step(): prob_low = attn_prob.astype(jnp.bfloat16)]
  transfers between devices with their start and end apart: 3 -> 0, of which waited for: 2 -> 0; matrix products, arithmetic and copies ran while one was open for 22% -> 0% of each run, Pallas kernels for 0% -> 0%
where the time goes in v1:
time: 75.9 us; the launch traced here: 75.5 us
  Pallas kernels  65.4 us (86%)
  local copies, waits for them, and re-layouts  7.46 us (10%)
  other arithmetic  1.99 us (3%)
    pallas_call x1, Pallas kernels, per_device(): pl.pallas_call(functools.partial(kernel, sizes), out_shape=(jax.ShapeDtyp...  65.4 us
    unnamed x4, local copies, waits for them, and re-layouts  3.05 us
    another operation x2, local copies, waits for them, and re-layouts, per_device(): prompt = jnp.stack((prompt_key, prompt_value_rows), axis=0)  1.53 us

profile of v1, /device:TPU:1, one launch (start us, length us, event | category | flops | bytes accessed | tf_op | source)
XLA Modules:
  0.0 75.5 jit_solution(7233082591237433268)
XLA Ops:
  0.6 0.8 %copy.18 = bf16[1,4,16,2,128]{4,2,3,0,1:T(8,128)(2,1)S(1)} copy(bf16[1,4,16,2,128]{4,3,2,1,0:T(2,128)(2,1)} %bitcast.22) | data formatting | bytes 65536 | tf_op jit(solution)/shard_map/stack | solution.py:479
  1.4 0.8 %copy.19 = bf16[1,4,16,2,128]{4,2,3,0,1:T(8,128)(2,1)S(1)} copy(bf16[1,4,16,2,128]{4,3,2,1,0:T(2,128)(2,1)} %bitcast.23) | data formatting | bytes 65536 | tf_op jit(solution)/shard_map/stack | solution.py:479
  2.2 0.6 maximum_bitcast_fusion.1.pr_ref
  2.8 1.4 %maximum_bitcast_fusion = bf16[2,2,2,128,128]{4,1,0,3,2:T(2,128)(2,1)S(1)} fusion(bf16[1,128,2,2,128]{4,3,2,1,0:T(2,128)(2,1)} %bitcast.20, bf16[1,128,2,2,128]{4,3,2,1,0:T(2,128)(2,1)} %bitcast.21), kind=kLoop, calls=%fused_computation | loop fusion | flops 131072 | bytes 524288 | tf_op jit(solution)/shard_map/transpose | solution.py:478
  4.2 0.7 copy.15
  4.9 65.4 %shard_map.120 = (bf16[128,2,16,128]{3,2,1,0:T(8,128)(2,1)}, bf16[4,2,128,128]{3,2,1,0:T(8,128)(2,1)}, bf16[64,2560]{1,0:T(8,128)(2,1)}) custom-call(s32[8]{0:T(128)} %len_ref.1, bf16[4,2,128,128]{3,2,1,0:T(8,128)(2,1)} %bitcast.17, bf16[4,2,2,16,128]{4,3,2,1,0:T(8,128)(2,1)} %maximum_bitcast_fusion.1.pr_ref, bf16[128,2,16,128]{3,2,1,0:T(8,128)(2,1)} %q_ref.1, ...), custom_call_target="tpu_custom_call" | custom-call | tf_op jit(solution)/shard_map/pallas_call | solution.py:527
  70.3 0.0 copy-start
  70.3 1.3 %copy.26 = bf16[2,2,2,128,128]{4,1,0,3,2:T(2,128)(2,1)S(1)} copy(bf16[2,2,2,128,128]{4,3,2,1,0:T(8,128)(2,1)} %bitcast.19) | data formatting | bytes 524288 | tf_op jit(solution)/shard_map/reshape | solution.py:549
  71.6 0.9 %slice_bitcast_fusion = (bf16[128,2,2,128]{3,2,1,0:T(2,128)(2,1)}, bf16[128,2,2,128]{3,2,1,0:T(2,128)(2,1)}) fusion(bf16[2,128,2,2,128]{4,3,2,1,0:T(2,128)(2,1)S(1)} %bitcast.18), kind=kLoop, calls=%fused_computation.2 | loop fusion | bytes 524288 | tf_op jit(solution)/shard_map/squeeze | solution.py:550
  72.5 2.3 %copy.29 = bf16[128,2,16,128]{3,2,1,0:T(8,128)(2,1)} copy(bf16[128,2,16,128]{3,2,1,0:T(8,128)(2,1)} %get-tuple-element.16) | data formatting | bytes 2097152
  74.8 0.0 copy-done
  74.8 0.7 copy.30
Async XLA Ops:
  70.3 4.5 %copy-start = (bf16[64,2560]{1,0:T(8,128)(2,1)S(1)}, bf16[64,2560]{1,0:T(8,128)(2,1)}, u32[]{:S(2)}) copy-start(bf16[64,2560]{1,0:T(8,128)(2,1)} %get-tuple-element.19) | copy-start | bytes 983044

commit v2 on v1

--- a/solution.py
+++ b/solution.py
@@ -24,17 +24,28 @@
 def kernel(
     sizes,
     len_ref,
+    key_ref,
+    value_ref,
+    pkey_ref,
+    pvalue_ref,
+    q_hbm,
+    cot_hbm,
+    km_ref,
+    vm_ref,
+    dq_hbm,
+    dkey_ref,
+    dvalue_ref,
+    out_ref,
+    q_ref,
+    cot_ref,
+    dq_ref,
+    wide,
     kv_ref,
     pr_ref,
-    q_ref,
-    cot_ref,
-    km_ref,
-    vm_ref,
-    dq_ref,
-    dkv_ref,
-    out_ref,
     qs,
     cots,
+    qts,
+    cotts,
     kv_all,
     pr_all,
     m_ref,
@@ -56,6 +67,7 @@
     xr,
     og,
     w_sem,
+    q_sem,
     c_send,
     c_recv,
     a_send,
@@ -122,8 +134,26 @@
                 )
         return copies
 
+    in_copies = (
+        pltpu.make_async_copy(q_hbm, q_ref, q_sem.at[0]),
+        pltpu.make_async_copy(cot_hbm, cot_ref, q_sem.at[1]),
+    )
+    out_copy = pltpu.make_async_copy(dq_ref, dq_hbm, q_sem.at[2])
+    for copy in in_copies:
+        copy.start()
     for copy in weight_copies():
         copy.start()
+
+    for which, ref in enumerate((key_ref, value_ref)):
+        wide[which] = ref[...].astype(jnp.float32)
+        for i in range(pairs):
+            kv_ref[i, which] = wide[which, pl.ds(i, L, stride=pairs), :].astype(jnp.bfloat16)
+    for which, ref in enumerate((pkey_ref, pvalue_ref)):
+        wide[which, : G * piece * H] = ref[...].astype(jnp.float32)
+        for gg in range(G):
+            for h in range(H):
+                rows_of = pl.ds(gg * piece * H + h, piece, stride=H)
+                pr_ref[gg, which, h] = wide[which, rows_of, :].astype(jnp.bfloat16)
 
     pl.semaphore_wait(barrier, n + G + T - 3)
 
@@ -146,18 +176,23 @@
         prompt_a(o).start()
 
     pos = p * L + lax.broadcasted_iota(jnp.int32, (L, F, E), 0)
+    for copy in in_copies:
+        copy.wait()
     for r in range(R):
         length = len_ref[g * R + r]
         q = q_ref[:, r].astype(jnp.float32)
         c = cot_ref[:, r].astype(jnp.float32)
         for h in range(H):
-            qs[r * H + h] = q[:, h * F : (h + 1) * F].reshape(rows, E).astype(jnp.bfloat16)
-            live = jnp.where(pos < length, c[:, h * F : (h + 1) * F], 0.0)
-            cots[r * H + h] = live.reshape(rows, E).astype(jnp.bfloat16)
+            part = q[:, h * F : (h + 1) * F].reshape(rows, E)
+            qs[r * H + h] = part.astype(jnp.bfloat16)
+            qts[r * H + h] = part.T.astype(jnp.bfloat16)
+            live = jnp.where(pos < length, c[:, h * F : (h + 1) * F], 0.0).reshape(rows, E)
+            cots[r * H + h] = live.astype(jnp.bfloat16)
+            cotts[r * H + h] = live.T.astype(jnp.bfloat16)
     pr_all[p] = pr_ref[...]
 
     def scores(pair, k, diag):
-        s = dot_nt(k, qs[pair]) * log_scale
+        s = dot_nn(k, qts[pair]) * log_scale
         if diag:
             key = lax.broadcasted_iota(jnp.int32, s.shape, 0)
             query = lax.broadcasted_iota(jnp.int32, s.shape, 1) // F
@@ -166,7 +201,7 @@
 
     def stats(pair, k, v, diag):
         s = scores(pair, k, diag)
-        dp = dot_nt(v, cots[pair])
+        dp = dot_nn(v, cotts[pair])
         if diag:
             m_new = jnp.max(s, axis=0, keepdims=True)
             e = jnp.exp2(s - m_new)
@@ -181,12 +216,18 @@
             d_ref[pair] = d_ref[pair] * a + jnp.sum(e * dp, axis=0, keepdims=True)
         m_ref[pair] = m_new
 
-    def each_pair(body):
+    together = 2 if pairs % 2 == 0 else 1
+
+    def each_pair(body, after=None):
         def step(i, carry):
-            body(i)
+            for k in range(together):
+                body(i * together + k)
+            if after is not None:
+                for k in range(together):
+                    after(i * together + k)
             return carry
 
-        lax.fori_loop(0, pairs, step, 0)
+        lax.fori_loop(0, pairs // together, step, 0)
 
     def prompt_block(which, pair):
         return pr_all[:, :, which, lax.rem(pair, H)].reshape(n * G * piece, E)
@@ -240,7 +281,7 @@
 
     def grads(pair, k, v, diag):
         prob = jnp.exp2(scores(pair, k, diag) - m_ref[pair])
-        dp = dot_nt(v, cots[pair])
+        dp = dot_nn(v, cotts[pair])
         ds = (prob * (dp - d_ref[pair])).astype(jnp.bfloat16)
         dv = dot_nn(prob.astype(jnp.bfloat16), cots[pair])
         dk = dot_nn(ds, qs[pair]) * scale
@@ -255,19 +296,17 @@
     def chunk_grads(j, carry):
         def body(i):
             dk, dv = grads(i, kv_all[j, i, 0], kv_all[j, i, 1], False)
-
+            gsend[j, i, 0] = dk.astype(jnp.bfloat16)
+            gsend[j, i, 1] = dv.astype(jnp.bfloat16)
+            own[j, i, 0] = dk
+            own[j, i, 1] = dv
+
+        def after(i):
             @pl.when(p == n - 1)
             def _():
-                gsend[j, i, 0] = dk.astype(jnp.bfloat16)
-                gsend[j, i, 1] = dv.astype(jnp.bfloat16)
                 grad_copy(j, i).start()
 
-            @pl.when(p < n - 1)
-            def _():
-                own[j, i, 0] = dk
-                own[j, i, 1] = dv
-
-        each_pair(body)
+        each_pair(body, after)
         return carry
 
     lax.fori_loop(0, jnp.minimum(p, 1), chunk_grads, 0)
@@ -297,22 +336,7 @@
     for o in range(1, G):
         r1(o).start()
 
-    lax.fori_loop(1, p, chunk_grads, 0)
-
-    def own_grads(i):
-        dk, dv = grads(i, kv_ref[i, 0], kv_ref[i, 1], True)
-
-        @pl.when(p == n - 1)
-        def _():
-            dkv_ref[i, 0] = dk.astype(jnp.bfloat16)
-            dkv_ref[i, 1] = dv.astype(jnp.bfloat16)
-
-        @pl.when(p < n - 1)
-        def _():
-            own[p, i, 0] = dk
-            own[p, i, 1] = dv
-
-    each_pair(own_grads)
+    lax.fori_loop(1, p - 1, chunk_grads, 0)
 
     for o in range(1, G):
         r1_wait(o)
@@ -332,9 +356,7 @@
     for o in range(1, n):
         r2(o).start()
 
-    for r in range(R):
-        parts = [dq_acc[r * H + h].T.reshape(L, F, E) for h in range(H)]
-        dq_ref[:, r] = (jnp.concatenate(parts, axis=1) * scale).astype(jnp.bfloat16)
+    lax.fori_loop(jnp.maximum(p - 1, 1), p, chunk_grads, 0)
 
     def relay(slot):
         j = slot - (n - 1 - p)
@@ -344,16 +366,15 @@
             def body(i):
                 grad_copy(j, i).wait_recv()
                 total = own[j, i] + grecv[j, i].astype(jnp.float32)
-                low = total.astype(jnp.bfloat16)
 
                 @pl.when(j < p)
                 def _():
-                    gsend[j, i] = low
+                    gsend[j, i] = total.astype(jnp.bfloat16)
                     grad_copy(j, i).start()
 
                 @pl.when(j == p)
                 def _():
-                    dkv_ref[i] = low
+                    own[j, i] = total
 
             each_pair(body)
 
@@ -377,6 +398,14 @@
 
     for o in range(1, G):
         r3(o).start()
+
+    def own_grads(i):
+        dk, dv = grads(i, kv_ref[i, 0], kv_ref[i, 1], True)
+        own[p, i, 0] = dk
+        own[p, i, 1] = dv
+
+    each_pair(own_grads)
+
     for copy in weight_copies():
         copy.wait()
     for o in range(1, G):
@@ -400,6 +429,11 @@
         x_copy(o).start()
     opart[...] = project(t)
 
+    for r in range(R):
+        parts = [dq_acc[r * H + h].T.reshape(L, F, E) for h in range(H)]
+        dq_ref[:, r] = (jnp.concatenate(parts, axis=1) * scale).astype(jnp.bfloat16)
+    out_copy.start()
+
     if n > 2:
         relay(n - 2)
 
@@ -420,10 +454,15 @@
     for o in range(1, G):
         o_copy(o).start()
     relay(n - 1)
+    for which, ref in enumerate((dkey_ref, dvalue_ref)):
+        for i in range(pairs):
+            wide[which, pl.ds(i, L, stride=pairs), :] = own[p, i, which]
+        ref[...] = wide[which].astype(jnp.bfloat16)
     for o in range(1, G):
         o_wait(o)
     for gg in range(G):
         out_ref[:, gg * quarter : (gg + 1) * quarter] = og[gg]
+    out_copy.wait()
 
     def chunk_sent(j, carry):
         chunk_copy(kv_ref, j).wait_send()
@@ -449,6 +488,15 @@
         o_copy(o).wait_send()
     for o in range(1, T):
         x_copy(o).wait_send()
+
+
+def hand_on(*refs):
+    sem = refs[8]
+    copies = [pltpu.make_async_copy(refs[i], refs[4 + i], sem.at[i]) for i in range(4)]
+    for copy in copies:
+        copy.start()
+    for copy in copies:
+        copy.wait()
 
 
 def per_device(
@@ -474,16 +522,20 @@
     quarter = width // T // G
     bf16, f32 = jnp.bfloat16, jnp.float32
 
-    kv = jnp.stack((response_key, response_value), axis=0)
-    kv = kv.transpose(2, 3, 0, 1, 4).reshape(pairs, 2, L, E)
-    prompt = jnp.stack((prompt_key, prompt_value_rows), axis=0)
-    prompt = prompt.reshape(2, G, piece, H, E).transpose(1, 0, 3, 2, 4)
-
     vmem = pl.BlockSpec(memory_space=pltpu.VMEM)
+    anywhere = pl.BlockSpec(memory_space=pl.ANY)
     dma = pltpu.SemaphoreType.DMA
     scratch = [
+        pltpu.VMEM((L, R, heads, E), bf16),
+        pltpu.VMEM((L, R, heads, E), bf16),
+        pltpu.VMEM((L, R, heads, E), bf16),
+        pltpu.VMEM((2, max(L * pairs, prompt_rows * H), E), f32),
+        pltpu.VMEM((pairs, 2, L, E), bf16),
+        pltpu.VMEM((G, 2, H, piece, E), bf16),
         pltpu.VMEM((pairs, rows, E), bf16),
         pltpu.VMEM((pairs, rows, E), bf16),
+        pltpu.VMEM((pairs, E, rows), bf16),
+        pltpu.VMEM((pairs, E, rows), bf16),
         pltpu.VMEM((n, pairs, 2, L, E), bf16),
         pltpu.VMEM((n, G, 2, H, piece, E), bf16),
         pltpu.VMEM((pairs, 1, rows), f32),
@@ -505,6 +557,7 @@
         pltpu.VMEM((max(T - 1, 1), prompt_rows, quarter), bf16),
         pltpu.VMEM((G, prompt_rows, quarter), bf16),
         dma((2, T)),
+        dma((3,)),
         dma((n,)),
         dma((n,)),
         dma((n,)),
@@ -524,30 +577,41 @@
         dma((G,)),
         dma((G,)),
     ]
-    query_grad, kv_grad, out = pl.pallas_call(
+    results = pl.pallas_call(
         functools.partial(kernel, sizes),
         out_shape=(
             jax.ShapeDtypeStruct((L, R, heads, E), bf16),
-            jax.ShapeDtypeStruct((pairs, 2, L, E), bf16),
+            jax.ShapeDtypeStruct((L * pairs, E), bf16),
+            jax.ShapeDtypeStruct((L * pairs, E), bf16),
             jax.ShapeDtypeStruct((prompt_rows, width // T), bf16),
         ),
-        in_specs=[
-            pl.BlockSpec(memory_space=pltpu.SMEM),
-            vmem,
-            vmem,
-            vmem,
-            vmem,
-            pl.BlockSpec(memory_space=pl.ANY),
-            pl.BlockSpec(memory_space=pl.ANY),
-        ],
-        out_specs=(vmem, vmem, vmem),
+        in_specs=[pl.BlockSpec(memory_space=pltpu.SMEM)] + [vmem] * 4 + [anywhere] * 4,
+        out_specs=(anywhere, vmem, vmem, vmem),
         scratch_shapes=scratch,
         compiler_params=pltpu.CompilerParams(
             collective_id=0, has_side_effects=True, vmem_limit_bytes=60 * 1024 * 1024
         ),
-    )(resp_lengths, kv, prompt, resp_query, resp_cotangent, key_matrix, value_matrix)
-    kv_grad = kv_grad.reshape(R, H, 2, L, E).transpose(2, 3, 0, 1, 4)
-    return (query_grad, kv_grad[0], kv_grad[1], out)
+    )(
+        resp_lengths,
+        response_key.reshape(L * pairs, E),
+        response_value.reshape(L * pairs, E),
+        prompt_key.reshape(prompt_rows * H, E),
+        prompt_value_rows.reshape(prompt_rows * H, E),
+        resp_query,
+        resp_cotangent,
+        key_matrix,
+        value_matrix,
+    )
+    query_grad, key_grad, value_grad, out = pl.pallas_call(
+        hand_on,
+        out_shape=tuple(jax.ShapeDtypeStruct(x.shape, x.dtype) for x in results),
+        in_specs=[anywhere] * 4,
+        out_specs=(anywhere,) * 4,
+        scratch_shapes=[dma((4,))],
+        compiler_params=pltpu.CompilerParams(vmem_limit_bytes=60 * 1024 * 1024),
+    )(*results)
+    shape = response_key.shape
+    return (query_grad, key_grad.reshape(shape), value_grad.reshape(shape), out)
 
 
 def solution(mesh):

time: 75.9 us -> 110 us (1.45)
  Pallas kernels: 65.4 us -> 109 us
  local copies, waits for them, and re-layouts: 7.46 us -> 0 us
  other arithmetic: 1.99 us -> 0 us
    pallas_call x0 -> x1, Pallas kernels: none -> 50.8 us  [per_device(): pl.pallas_call(hand_on, out_shape=tuple((jax.ShapeDtypeStruct(x.shape, x....]
    pallas_call x1, Pallas kernels: 65.4 us -> 58.6 us  [per_device(): pl.pallas_call(functools.partial(kernel, sizes), out_shape=(jax.ShapeDtyp...]
    unnamed x4 -> x0, local copies, waits for them, and re-layouts: 3.05 us -> none
    transpose x2 -> x0, other arithmetic: 1.99 us -> none  [the longest x1 1.36 us: per_device(): kv = kv.transpose(2, 3, 0, 1, 4).reshape(pairs, 2, L, E)]
    another operation x2 -> x0, local copies, waits for them, and re-layouts: 1.53 us -> none  [per_device(): prompt = jnp.stack((prompt_key, prompt_value_rows), axis=0)]
    reshape x1 -> x0, local copies, waits for them, and re-layouts: 1.27 us -> none  [per_device(): kv_grad = kv_grad.reshape(R, H, 2, L, E).transpose(2, 3, 0, 1, 4)]
where the time goes in v2:
time: 110 us
  Pallas kernels  109 us (99%)
    pallas_call x1, Pallas kernels, per_device(): pl.pallas_call(functools.partial(kernel, sizes), out_shape=(jax.ShapeDtyp...  58.6 us
    pallas_call x1, Pallas kernels, per_device(): pl.pallas_call(hand_on, out_shape=tuple((jax.ShapeDtypeStruct(x.shape, x....  50.8 us

profile of v2, /device:TPU:1, one launch (start us, length us, event | category | flops | bytes accessed | tf_op | source)
XLA Modules:
  0.0 110.0 jit_solution(1370333659665739880)
XLA Ops:
  0.6 58.6 %shard_map.120 = (bf16[128,2,16,128]{3,2,1,0:T(8,128)(2,1)}, bf16[512,128]{1,0:T(8,128)(2,1)}, bf16[512,128]{1,0:T(8,128)(2,1)}, bf16[64,2560]{1,0:T(8,128)(2,1)}) custom-call(s32[8]{0:T(128)} %len_ref.1, bf16[512,128]{1,0:T(8,128)(2,1)} %bitcast.6, bf16[512,128]{1,0:T(8,128)(2,1)} %bitcast.7, bf16[128,128]{1,0:T(8,128)(2,1)} %bitcast.8, ...), custom_call_target="tpu_custom_call" | custom-call | tf_op jit(solution)/shard_map/pallas_call | solution.py:580
  59.3 50.8 %shard_map.121 = (bf16[128,2,16,128]{3,2,1,0:T(8,128)(2,1)}, bf16[512,128]{1,0:T(8,128)(2,1)}, bf16[512,128]{1,0:T(8,128)(2,1)}, bf16[64,2560]{1,0:T(8,128)(2,1)}) custom-call(bf16[128,2,16,128]{3,2,1,0:T(8,128)(2,1)} %get-tuple-element.12.refs_0_, bf16[512,128]{1,0:T(8,128)(2,1)} %get-tuple-element.13.refs_1_, bf16[512,128]{1,0:T(8,128)(2,1)} %get-tuple-element.14.refs_2_, ...), custom_call_target="tpu_custom_call" | custom-call | tf_op jit(solution)/shard_map/pallas_call | solution.py:605

commit v3 on v2

--- a/solution.py
+++ b/solution.py
@@ -48,6 +48,8 @@
     cotts,
     kv_all,
     pr_all,
+    s_buf,
+    dp_buf,
     m_ref,
     l_ref,
     d_ref,
@@ -145,7 +147,7 @@
         copy.start()
 
     for which, ref in enumerate((key_ref, value_ref)):
-        wide[which] = ref[...].astype(jnp.float32)
+        wide[which, : L * pairs] = ref[...].astype(jnp.float32)
         for i in range(pairs):
             kv_ref[i, which] = wide[which, pl.ds(i, L, stride=pairs), :].astype(jnp.bfloat16)
     for which, ref in enumerate((pkey_ref, pvalue_ref)):
@@ -157,12 +159,14 @@
 
     pl.semaphore_wait(barrier, n + G + T - 3)
 
-    def chunk_copy(src, j):
-        return remote(src, kv_all.at[j], c_send.at[j], c_recv.at[j], at(pp=lax.rem(p + 1, n)))
-
-    @pl.when(p < n - 1)
-    def _():
-        chunk_copy(kv_ref, p).start()
+    def order(k):
+        return lax.rem(k, R) * H + k // R
+
+    def chunk_copy(dest, i):
+        return remote(kv_ref.at[i], kv_all.at[p, i], c_send.at[dest, i], c_recv.at[p, i], at(pp=dest))
+
+    def chunk_wait(j, i):
+        remote(kv_ref.at[i], kv_all.at[j, i], c_send.at[j, i], c_recv.at[j, i], at(pp=j)).wait_recv()
 
     def prompt_a(o):
         dest = peer(p, o, n)
@@ -175,6 +179,28 @@
     for o in range(1, n):
         prompt_a(o).start()
 
+    def send_pair(k, carry):
+        def send_to(d, inner):
+            chunk_copy(n - 1 - d, order(k)).start()
+            return inner
+
+        return lax.fori_loop(0, n - 1 - p, send_to, carry)
+
+    lax.fori_loop(0, pairs, send_pair, 0)
+
+    def prompt_b(o, oo):
+        src, dest = peer(p, o, n), peer(g, oo, G)
+        return remote(
+            pr_all.at[src, g], pr_all.at[src, g], b_send.at[dest, src], b_recv.at[g, src], at(gg=dest)
+        )
+
+    def prompt_b_wait(o, oo):
+        src, frm = peer(p, o, n), peer(g, oo, G)
+        remote(
+            pr_all.at[src, frm], pr_all.at[src, frm], b_send.at[frm, src], b_recv.at[frm, src], at(gg=frm)
+        ).wait_recv()
+
+    pr_all[p] = pr_ref[...]
     pos = p * L + lax.broadcasted_iota(jnp.int32, (L, F, E), 0)
     for copy in in_copies:
         copy.wait()
@@ -189,198 +215,147 @@
             live = jnp.where(pos < length, c[:, h * F : (h + 1) * F], 0.0).reshape(rows, E)
             cots[r * H + h] = live.astype(jnp.bfloat16)
             cotts[r * H + h] = live.T.astype(jnp.bfloat16)
-    pr_all[p] = pr_ref[...]
-
-    def scores(pair, k, diag):
+        if r == 0:
+            for o in range(1, n):
+                prompt_a_wait(o)
+                for oo in range(1, G):
+                    prompt_b(o, oo).start()
+    for o in range(1, n):
+        for oo in range(1, G):
+            prompt_b_wait(o, oo)
+
+    prompt_keys = n * G * piece
+
+    def prompt_block(which, pair):
+        return pr_all[:, :, which, lax.rem(pair, H)].reshape(prompt_keys, E)
+
+    def block(j):
+        return pl.ds(pl.multiple_of(j * L, L), L)
+
+    prompt_rows = pl.ds(n * L, prompt_keys)
+
+    def stats(pair, where, k, v, diag):
         s = dot_nn(k, qts[pair]) * log_scale
         if diag:
             key = lax.broadcasted_iota(jnp.int32, s.shape, 0)
             query = lax.broadcasted_iota(jnp.int32, s.shape, 1) // F
             s = jnp.where(key <= query, s, masked_score)
-        return s
-
-    def stats(pair, k, v, diag):
-        s = scores(pair, k, diag)
         dp = dot_nn(v, cotts[pair])
+        s_buf[where, :] = s
+        dp_buf[where, :] = dp
+        top = jnp.max(s, axis=0, keepdims=True)
         if diag:
-            m_new = jnp.max(s, axis=0, keepdims=True)
-            e = jnp.exp2(s - m_new)
-            l_ref[pair] = jnp.sum(e, axis=0, keepdims=True)
-            d_ref[pair] = jnp.sum(e * dp, axis=0, keepdims=True)
+            e = jnp.exp2(s - top)
+            l_ref[...] = jnp.sum(e, axis=0, keepdims=True)
+            d_ref[...] = jnp.sum(e * dp, axis=0, keepdims=True)
+            m_ref[...] = top
         else:
-            m_old = m_ref[pair]
-            m_new = jnp.maximum(m_old, jnp.max(s, axis=0, keepdims=True))
+            m_old = m_ref[...]
+            m_new = jnp.maximum(m_old, top)
             e = jnp.exp2(s - m_new)
             a = jnp.exp2(m_old - m_new)
-            l_ref[pair] = l_ref[pair] * a + jnp.sum(e, axis=0, keepdims=True)
-            d_ref[pair] = d_ref[pair] * a + jnp.sum(e * dp, axis=0, keepdims=True)
-        m_ref[pair] = m_new
-
-    together = 2 if pairs % 2 == 0 else 1
-
-    def each_pair(body, after=None):
-        def step(i, carry):
-            for k in range(together):
-                body(i * together + k)
-            if after is not None:
-                for k in range(together):
-                    after(i * together + k)
-            return carry
-
-        lax.fori_loop(0, pairs // together, step, 0)
-
-    def prompt_block(which, pair):
-        return pr_all[:, :, which, lax.rem(pair, H)].reshape(n * G * piece, E)
-
-    each_pair(lambda i: stats(i, kv_ref[i, 0], kv_ref[i, 1], True))
-
-    def prompt_b(o, oo):
-        src, dest = peer(p, o, n), peer(g, oo, G)
-        return remote(
-            pr_all.at[src, g], pr_all.at[src, g], b_send.at[dest, src], b_recv.at[g, src], at(gg=dest)
-        )
-
-    def prompt_b_wait(o, oo):
-        src, frm = peer(p, o, n), peer(g, oo, G)
-        remote(
-            pr_all.at[src, frm], pr_all.at[src, frm], b_send.at[frm, src], b_recv.at[frm, src], at(gg=frm)
-        ).wait_recv()
-
-    for o in range(1, n):
-        prompt_a_wait(o)
-        for oo in range(1, G):
-            prompt_b(o, oo).start()
-
-    def prompt_stats():
-        for o in range(1, n):
-            for oo in range(1, G):
-                prompt_b_wait(o, oo)
-        each_pair(lambda i: stats(i, prompt_block(0, i), prompt_block(1, i), False))
-
-    def chunk_step(s, carry):
-        j = p - s
-        chunk_copy(kv_ref, j).wait_recv()
-
-        @pl.when(p < n - 1)
-        def _():
-            chunk_copy(kv_all.at[j], j).start()
-
-        each_pair(lambda i: stats(i, kv_all[j, i, 0], kv_all[j, i, 1], False))
-        return carry
-
-    lax.fori_loop(1, jnp.minimum(p, 1) + 1, chunk_step, 0)
-    prompt_stats()
-    lax.fori_loop(2, p + 1, chunk_step, 0)
-
-    def finish(i):
-        d_ref[i] = d_ref[i] / l_ref[i]
-        m_ref[i] = m_ref[i] + jnp.log(l_ref[i]) * log2_e
-        dq_acc[i] = jnp.zeros((E, rows), jnp.float32)
-
-    each_pair(finish)
-
-    def grads(pair, k, v, diag):
-        prob = jnp.exp2(scores(pair, k, diag) - m_ref[pair])
-        dp = dot_nn(v, cotts[pair])
-        ds = (prob * (dp - d_ref[pair])).astype(jnp.bfloat16)
+            l_ref[...] = l_ref[...] * a + jnp.sum(e, axis=0, keepdims=True)
+            d_ref[...] = d_ref[...] * a + jnp.sum(e * dp, axis=0, keepdims=True)
+            m_ref[...] = m_new
+
+    def grads(pair, where, k, first=False):
+        prob = jnp.exp2(s_buf[where, :] - m_ref[...])
+        ds = (prob * (dp_buf[where, :] - d_ref[...])).astype(jnp.bfloat16)
         dv = dot_nn(prob.astype(jnp.bfloat16), cots[pair])
         dk = dot_nn(ds, qs[pair]) * scale
-        dq_acc[pair] += dot_nn(k.T, ds)
+        term = dot_nn(k.T, ds)
+        if first:
+            dq_acc[pair] = term
+        else:
+            dq_acc[pair] += term
         return dk, dv
 
     def grad_copy(j, i):
-        return remote(
-            gsend.at[j, i], grecv.at[j, i], g_send.at[j, i], g_recv.at[j, i], at(pp=lax.rem(p + n - 1, n))
-        )
-
-    def chunk_grads(j, carry):
-        def body(i):
-            dk, dv = grads(i, kv_all[j, i, 0], kv_all[j, i, 1], False)
-            gsend[j, i, 0] = dk.astype(jnp.bfloat16)
-            gsend[j, i, 1] = dv.astype(jnp.bfloat16)
-            own[j, i, 0] = dk
-            own[j, i, 1] = dv
-
-        def after(i):
-            @pl.when(p == n - 1)
-            def _():
-                grad_copy(j, i).start()
-
-        each_pair(body, after)
-        return carry
-
-    lax.fori_loop(0, jnp.minimum(p, 1), chunk_grads, 0)
+        return remote(gsend.at[j, i], grecv.at[p, i], g_send.at[j, i], g_recv.at[p, i], at(pp=j))
+
+    def grad_wait(j, i):
+        remote(gsend.at[j, i], grecv.at[j, i], g_send.at[j, i], g_recv.at[j, i], at(pp=j)).wait_recv()
+
+    def r1(o):
+        dest = peer(g, o, G)
+        return remote(ps1.at[dest], pr1.at[g], r1_send.at[dest], r1_recv.at[g], at(gg=dest))
+
+    def r1_wait(o):
+        src = peer(g, o, G)
+        remote(ps1.at[src], pr1.at[src], r1_send.at[src], r1_recv.at[src], at(gg=src)).wait_recv()
+
+    def r2(o):
+        dest = peer(p, o, n)
+        return remote(ps2.at[dest], pr2.at[p], r2_send.at[dest], r2_recv.at[p], at(pp=dest))
+
+    def r2_wait(o):
+        src = peer(p, o, n)
+        remote(ps2.at[src], pr2.at[src], r2_send.at[src], r2_recv.at[src], at(pp=src)).wait_recv()
 
     pacc[...] = jnp.zeros_like(pacc)
 
-    def prompt_grads(i):
-        dk, dv = grads(i, prompt_block(0, i), prompt_block(1, i), False)
+    def one_pair(step, carry):
+        i = order(step)
+        stats(i, block(p), kv_ref[i, 0], kv_ref[i, 1], True)
+        stats(i, prompt_rows, prompt_block(0, i), prompt_block(1, i), False)
+
+        def chunk_stats(o, inner):
+            j = p - o
+            chunk_wait(j, i)
+            stats(i, block(j), kv_all[j, i, 0], kv_all[j, i, 1], False)
+            return inner
+
+        lax.fori_loop(1, p + 1, chunk_stats, 0)
+        d_ref[...] = d_ref[...] / l_ref[...]
+        m_ref[...] = m_ref[...] + jnp.log(l_ref[...]) * log2_e
+
         h = lax.rem(i, H)
+        dk, dv = grads(i, prompt_rows, prompt_block(0, i), True)
         dk = dk.reshape(n, G, piece, E)
         dv = dv.reshape(n, G, piece, E)
         for gg in range(G):
             pacc[gg, :, 0, h] += dk[:, gg]
             pacc[gg, :, 1, h] += dv[:, gg]
 
-    each_pair(prompt_grads)
-    ps1[...] = pacc[...].astype(jnp.bfloat16)
-
-    def r1(o):
-        dest = peer(g, o, G)
-        return remote(ps1.at[dest], pr1.at[g], r1_send.at[dest], r1_recv.at[g], at(gg=dest))
-
-    def r1_wait(o):
-        src = peer(g, o, G)
-        remote(ps1.at[src], pr1.at[src], r1_send.at[src], r1_recv.at[src], at(gg=src)).wait_recv()
-
-    for o in range(1, G):
-        r1(o).start()
-
-    lax.fori_loop(1, p - 1, chunk_grads, 0)
-
-    for o in range(1, G):
-        r1_wait(o)
-    pacc[g] = functools.reduce(
-        lambda a, b: a + b, [pr1[peer(g, o, G)].astype(jnp.float32) for o in range(1, G)], pacc[g]
-    )
-    ps2[...] = pacc[g].astype(jnp.bfloat16)
-
-    def r2(o):
-        dest = peer(p, o, n)
-        return remote(ps2.at[dest], pr2.at[p], r2_send.at[dest], r2_recv.at[p], at(pp=dest))
-
-    def r2_wait(o):
-        src = peer(p, o, n)
-        remote(ps2.at[src], pr2.at[src], r2_send.at[src], r2_recv.at[src], at(pp=src)).wait_recv()
-
-    for o in range(1, n):
-        r2(o).start()
-
-    lax.fori_loop(jnp.maximum(p - 1, 1), p, chunk_grads, 0)
-
-    def relay(slot):
-        j = slot - (n - 1 - p)
-
-        @pl.when((p < n - 1) & (j >= 0))
+        @pl.when(step == pairs - 1)
         def _():
-            def body(i):
-                grad_copy(j, i).wait_recv()
-                total = own[j, i] + grecv[j, i].astype(jnp.float32)
-
-                @pl.when(j < p)
-                def _():
-                    gsend[j, i] = total.astype(jnp.bfloat16)
-                    grad_copy(j, i).start()
-
-                @pl.when(j == p)
-                def _():
-                    own[j, i] = total
-
-            each_pair(body)
-
-    for slot in range(1, n - 2):
-        relay(slot)
-
+            ps1[...] = pacc[...].astype(jnp.bfloat16)
+            for o in range(1, G):
+                r1(o).start()
+
+        def chunk_grads(j, inner):
+            dk, dv = grads(i, block(j), kv_all[j, i, 0])
+            gsend[j, i, 0] = dk.astype(jnp.bfloat16)
+            gsend[j, i, 1] = dv.astype(jnp.bfloat16)
+            grad_copy(j, i).start()
+            return inner
+
+        lax.fori_loop(0, p, chunk_grads, 0)
+
+        @pl.when(step == pairs - 1)
+        def _():
+            for o in range(1, G):
+                r1_wait(o)
+            total = pacc[g]
+            for o in range(1, G):
+                total = total + pr1[peer(g, o, G)].astype(jnp.float32)
+            pacc[g] = total
+            ps2[...] = total.astype(jnp.bfloat16)
+            for o in range(1, n):
+                r2(o).start()
+
+        dk, dv = grads(i, block(p), kv_ref[i, 0])
+        own[i, 0] = dk
+        own[i, 1] = dv
+        return carry
+
+    lax.fori_loop(0, pairs, one_pair, 0)
+
+    def write_query_grad(r):
+        parts = [dq_acc[r * H + h].T.reshape(L, F, E) for h in range(H)]
+        dq_ref[:, r] = (jnp.concatenate(parts, axis=1) * scale).astype(jnp.bfloat16)
+
+    write_query_grad(0)
     for o in range(1, n):
         r2_wait(o)
     total = pacc[g, p]
@@ -398,14 +373,9 @@
 
     for o in range(1, G):
         r3(o).start()
-
-    def own_grads(i):
-        dk, dv = grads(i, kv_ref[i, 0], kv_ref[i, 1], True)
-        own[p, i, 0] = dk
-        own[p, i, 1] = dv
-
-    each_pair(own_grads)
-
+    for r in range(1, R):
+        write_query_grad(r)
+    out_copy.start()
     for copy in weight_copies():
         copy.wait()
     for o in range(1, G):
@@ -429,13 +399,15 @@
         x_copy(o).start()
     opart[...] = project(t)
 
-    for r in range(R):
-        parts = [dq_acc[r * H + h].T.reshape(L, F, E) for h in range(H)]
-        dq_ref[:, r] = (jnp.concatenate(parts, axis=1) * scale).astype(jnp.bfloat16)
-    out_copy.start()
-
-    if n > 2:
-        relay(n - 2)
+    def add_terms(i, carry):
+        def add_one(j, inner):
+            grad_wait(j, i)
+            own[i] += grecv[j, i].astype(jnp.float32)
+            return inner
+
+        return lax.fori_loop(p + 1, n, add_one, carry)
+
+    lax.fori_loop(0, pairs, add_terms, 0)
 
     result = opart[...]
     for o in range(1, T):
@@ -453,30 +425,29 @@
 
     for o in range(1, G):
         o_copy(o).start()
-    relay(n - 1)
     for which, ref in enumerate((dkey_ref, dvalue_ref)):
         for i in range(pairs):
-            wide[which, pl.ds(i, L, stride=pairs), :] = own[p, i, which]
-        ref[...] = wide[which].astype(jnp.bfloat16)
+            wide[which, pl.ds(i, L, stride=pairs), :] = own[i, which]
+        ref[...] = wide[which, : L * pairs].astype(jnp.bfloat16)
     for o in range(1, G):
         o_wait(o)
     for gg in range(G):
         out_ref[:, gg * quarter : (gg + 1) * quarter] = og[gg]
     out_copy.wait()
 
-    def chunk_sent(j, carry):
-        chunk_copy(kv_ref, j).wait_send()
-        return carry
-
-    @pl.when(p < n - 1)
-    def _():
-        lax.fori_loop(0, p + 1, chunk_sent, 0)
-
-    def grads_sent(j, carry):
-        each_pair(lambda i: grad_copy(j, i).wait_send())
-        return carry
-
-    lax.fori_loop(0, p, grads_sent, 0)
+    def pair_sent(i, carry):
+        def chunk_sent(j, inner):
+            chunk_copy(j, i).wait_send()
+            return inner
+
+        def grad_sent(j, inner):
+            grad_copy(j, i).wait_send()
+            return inner
+
+        lax.fori_loop(p + 1, n, chunk_sent, 0)
+        return lax.fori_loop(0, p, grad_sent, carry)
+
+    lax.fori_loop(0, pairs, pair_sent, 0)
     for o in range(1, n):
         prompt_a(o).wait_send()
         r2(o).wait_send()
@@ -491,11 +462,17 @@
 
 
 def hand_on(*refs):
-    sem = refs[8]
-    copies = [pltpu.make_async_copy(refs[i], refs[4 + i], sem.at[i]) for i in range(4)]
-    for copy in copies:
+    count = 4
+    sources, targets, held = refs[:count], refs[count : 2 * count], refs[2 * count : 3 * count]
+    in_sem, out_sem = refs[3 * count :]
+    arriving = [pltpu.make_async_copy(sources[i], held[i], in_sem.at[i]) for i in range(count)]
+    leaving = [pltpu.make_async_copy(held[i], targets[i], out_sem.at[i]) for i in range(count)]
+    for copy in arriving:
         copy.start()
-    for copy in copies:
+    for came, goes in zip(arriving, leaving):
+        came.wait()
+        goes.start()
+    for copy in leaving:
         copy.wait()
 
 
@@ -538,11 +515,13 @@
         pltpu.VMEM((pairs, E, rows), bf16),
         pltpu.VMEM((n, pairs, 2, L, E), bf16),
         pltpu.VMEM((n, G, 2, H, piece, E), bf16),
-        pltpu.VMEM((pairs, 1, rows), f32),
-        pltpu.VMEM((pairs, 1, rows), f32),
-        pltpu.VMEM((pairs, 1, rows), f32),
+        pltpu.VMEM((n * L + n * prompt_rows, rows), f32),
+        pltpu.VMEM((n * L + n * prompt_rows, rows), f32),
+        pltpu.VMEM((1, rows), f32),
+        pltpu.VMEM((1, rows), f32),
+        pltpu.VMEM((1, rows), f32),
         pltpu.VMEM((pairs, E, rows), f32),
-        pltpu.VMEM((n, pairs, 2, L, E), f32),
+        pltpu.VMEM((pairs, 2, L, E), f32),
         pltpu.VMEM((n, pairs, 2, L, E), bf16),
         pltpu.VMEM((n, pairs, 2, L, E), bf16),
         pltpu.VMEM((G, n, 2, H, piece, E), f32),
@@ -558,8 +537,8 @@
         pltpu.VMEM((G, prompt_rows, quarter), bf16),
         dma((2, T)),
         dma((3,)),
-        dma((n,)),
-        dma((n,)),
+        dma((n, pairs)),
+        dma((n, pairs)),
         dma((n,)),
         dma((n,)),
         dma((G, n)),
@@ -607,7 +586,7 @@
         out_shape=tuple(jax.ShapeDtypeStruct(x.shape, x.dtype) for x in results),
         in_specs=[anywhere] * 4,
         out_specs=(anywhere,) * 4,
-        scratch_shapes=[dma((4,))],
+        scratch_shapes=[pltpu.VMEM(x.shape, x.dtype) for x in results] + [dma((4,)), dma((4,))],
         compiler_params=pltpu.CompilerParams(vmem_limit_bytes=60 * 1024 * 1024),
     )(*results)
     shape = response_key.shape

time: 110 us -> 62.7 us (0.57)
  Pallas kernels: 109 us -> 61.9 us
    pallas_call x1, Pallas kernels: 50.8 us -> 2.45 us  [per_device(): pl.pallas_call(hand_on, out_shape=tuple((jax.ShapeDtypeStruct(x.shape, x....]
where the time goes in v3:
time: 62.7 us; the launch traced here: 62.5 us
  Pallas kernels  61.9 us (99%)
  between operations  0.64 us (1%)
    pallas_call x1, Pallas kernels, per_device(): pl.pallas_call(functools.partial(kernel, sizes), out_shape=(jax.ShapeDtyp...  59.4 us
    pallas_call x1, Pallas kernels, per_device(): pl.pallas_call(hand_on, out_shape=tuple((jax.ShapeDtypeStruct(x.shape, x....  2.45 us

profile of v3, /device:TPU:1, one launch (start us, length us, event | category | flops | bytes accessed | tf_op | source)
XLA Modules:
  0.0 62.5 jit_solution(2104306612477103390)
XLA Ops:
  0.6 59.4 %shard_map.120 = (bf16[128,2,16,128]{3,2,1,0:T(8,128)(2,1)}, bf16[512,128]{1,0:T(8,128)(2,1)}, bf16[512,128]{1,0:T(8,128)(2,1)}, bf16[64,2560]{1,0:T(8,128)(2,1)}) custom-call(s32[8]{0:T(128)} %len_ref.1, bf16[512,128]{1,0:T(8,128)(2,1)} %bitcast.6, bf16[512,128]{1,0:T(8,128)(2,1)} %bitcast.7, bf16[128,128]{1,0:T(8,128)(2,1)} %bitcast.8, ...), custom_call_target="tpu_custom_call" | custom-call | tf_op jit(solution)/shard_map/pallas_call | solution.py:559
  60.0 2.5 %shard_map.121 = (bf16[128,2,16,128]{3,2,1,0:T(8,128)(2,1)}, bf16[512,128]{1,0:T(8,128)(2,1)}, bf16[512,128]{1,0:T(8,128)(2,1)}, bf16[64,2560]{1,0:T(8,128)(2,1)}) custom-call(bf16[128,2,16,128]{3,2,1,0:T(8,128)(2,1)} %get-tuple-element.12.refs_0_, bf16[512,128]{1,0:T(8,128)(2,1)} %get-tuple-element.13.refs_1_, bf16[512,128]{1,0:T(8,128)(2,1)} %get-tuple-element.14.refs_2_, ...), custom_call_target="tpu_custom_call" | custom-call | tf_op jit(solution)/shard_map/pallas_call | solution.py:584

commit v4 on v3

--- a/solution.py
+++ b/solution.py
@@ -162,11 +162,31 @@
     def order(k):
         return lax.rem(k, R) * H + k // R
 
-    def chunk_copy(dest, i):
-        return remote(kv_ref.at[i], kv_all.at[p, i], c_send.at[dest, i], c_recv.at[p, i], at(pp=dest))
+    up, down = lax.rem(p + 1, n), lax.rem(p + n - 1, n)
+
+    def chunk_copy(src, j, i):
+        return remote(src, kv_all.at[j, i], c_send.at[j, i], c_recv.at[j, i], at(pp=up))
 
     def chunk_wait(j, i):
-        remote(kv_ref.at[i], kv_all.at[j, i], c_send.at[j, i], c_recv.at[j, i], at(pp=j)).wait_recv()
+        chunk_copy(kv_ref.at[i], j, i).wait_recv()
+
+    def send_own(k):
+        @pl.when((p < n - 1) & (k < pairs))
+        def _():
+            i = order(k)
+            chunk_copy(kv_ref.at[i], p, i).start()
+
+    def pass_on(k):
+        @pl.when((p < n - 1) & (k < pairs))
+        def _():
+            i = order(k)
+
+            def one(o, inner):
+                chunk_wait(p - o, i)
+                chunk_copy(kv_all.at[p - o, i], p - o, i).start()
+                return inner
+
+            lax.fori_loop(1, p + 1, one, 0)
 
     def prompt_a(o):
         dest = peer(p, o, n)
@@ -179,14 +199,8 @@
     for o in range(1, n):
         prompt_a(o).start()
 
-    def send_pair(k, carry):
-        def send_to(d, inner):
-            chunk_copy(n - 1 - d, order(k)).start()
-            return inner
-
-        return lax.fori_loop(0, n - 1 - p, send_to, carry)
-
-    lax.fori_loop(0, pairs, send_pair, 0)
+    send_own(0)
+    send_own(1)
 
     def prompt_b(o, oo):
         src, dest = peer(p, o, n), peer(g, oo, G)
@@ -271,10 +285,23 @@
         return dk, dv
 
     def grad_copy(j, i):
-        return remote(gsend.at[j, i], grecv.at[p, i], g_send.at[j, i], g_recv.at[p, i], at(pp=j))
-
-    def grad_wait(j, i):
-        remote(gsend.at[j, i], grecv.at[j, i], g_send.at[j, i], g_recv.at[j, i], at(pp=j)).wait_recv()
+        return remote(gsend.at[j, i], grecv.at[j, i], g_send.at[j, i], g_recv.at[j, i], at(pp=down))
+
+    def add_up(k):
+        i = order(k)
+
+        def one(j, inner):
+            grad_copy(j, i).wait_recv()
+            total = gsend[j, i].astype(jnp.float32) + grecv[j, i].astype(jnp.float32)
+            gsend[j, i] = total.astype(jnp.bfloat16)
+            grad_copy(j, i).start()
+            return inner
+
+        lax.fori_loop(0, p, one, 0)
+        grad_copy(p, i).wait_recv()
+        own[i] += grecv[p, i].astype(jnp.float32)
+
+    lag = n - 1 - p
 
     def r1(o):
         dest = peer(g, o, G)
@@ -296,12 +323,23 @@
 
     def one_pair(step, carry):
         i = order(step)
+
+        @pl.when(step == 0)
+        def _():
+            pass_on(0)
+
+        pass_on(step + 1)
+        send_own(step + 2)
         stats(i, block(p), kv_ref[i, 0], kv_ref[i, 1], True)
         stats(i, prompt_rows, prompt_block(0, i), prompt_block(1, i), False)
 
         def chunk_stats(o, inner):
             j = p - o
-            chunk_wait(j, i)
+
+            @pl.when(p == n - 1)
+            def _():
+                chunk_wait(j, i)
+
             stats(i, block(j), kv_all[j, i, 0], kv_all[j, i, 1], False)
             return inner
 
@@ -327,7 +365,11 @@
             dk, dv = grads(i, block(j), kv_all[j, i, 0])
             gsend[j, i, 0] = dk.astype(jnp.bfloat16)
             gsend[j, i, 1] = dv.astype(jnp.bfloat16)
-            grad_copy(j, i).start()
+
+            @pl.when(p == n - 1)
+            def _():
+                grad_copy(j, i).start()
+
             return inner
 
         lax.fori_loop(0, p, chunk_grads, 0)
@@ -347,6 +389,11 @@
         dk, dv = grads(i, block(p), kv_ref[i, 0])
         own[i, 0] = dk
         own[i, 1] = dv
+
+        @pl.when((lag > 0) & (step >= lag))
+        def _():
+            add_up(step - lag)
+
         return carry
 
     lax.fori_loop(0, pairs, one_pair, 0)
@@ -355,7 +402,12 @@
         parts = [dq_acc[r * H + h].T.reshape(L, F, E) for h in range(H)]
         dq_ref[:, r] = (jnp.concatenate(parts, axis=1) * scale).astype(jnp.bfloat16)
 
-    write_query_grad(0)
+    def add_rest(k, carry):
+        add_up(k)
+        return carry
+
+    left = jnp.maximum(pairs - lag, 0)
+
     for o in range(1, n):
         r2_wait(o)
     total = pacc[g, p]
@@ -373,7 +425,8 @@
 
     for o in range(1, G):
         r3(o).start()
-    for r in range(1, R):
+    lax.fori_loop(left, jnp.where(p > 0, pairs, left), add_rest, 0)
+    for r in range(R):
         write_query_grad(r)
     out_copy.start()
     for copy in weight_copies():
@@ -399,16 +452,6 @@
         x_copy(o).start()
     opart[...] = project(t)
 
-    def add_terms(i, carry):
-        def add_one(j, inner):
-            grad_wait(j, i)
-            own[i] += grecv[j, i].astype(jnp.float32)
-            return inner
-
-        return lax.fori_loop(p + 1, n, add_one, carry)
-
-    lax.fori_loop(0, pairs, add_terms, 0)
-
     result = opart[...]
     for o in range(1, T):
         x_copy(o).wait_recv()
@@ -425,6 +468,7 @@
 
     for o in range(1, G):
         o_copy(o).start()
+    lax.fori_loop(left, jnp.where(p > 0, left, pairs), add_rest, 0)
     for which, ref in enumerate((dkey_ref, dvalue_ref)):
         for i in range(pairs):
             wide[which, pl.ds(i, L, stride=pairs), :] = own[i, which]
@@ -437,14 +481,14 @@
 
     def pair_sent(i, carry):
         def chunk_sent(j, inner):
-            chunk_copy(j, i).wait_send()
+            chunk_copy(kv_ref.at[i], j, i).wait_send()
             return inner
 
         def grad_sent(j, inner):
             grad_copy(j, i).wait_send()
             return inner
 
-        lax.fori_loop(p + 1, n, chunk_sent, 0)
+        lax.fori_loop(0, jnp.where(p < n - 1, p + 1, 0), chunk_sent, 0)
         return lax.fori_loop(0, p, grad_sent, carry)
 
     lax.fori_loop(0, pairs, pair_sent, 0)

time: 62.7 us -> 60 us (0.957)
  the two profiles are of different devices: /device:TPU:1 before, /device:TPU:9 now
where the time goes in v4:
time: 60 us; the launch traced here: 59.8 us
  Pallas kernels  59.2 us (99%)
  between operations  0.64 us (1%)
    pallas_call x1, Pallas kernels, per_device(): pl.pallas_call(functools.partial(kernel, sizes), out_shape=(jax.ShapeDtyp...  56.7 us
    pallas_call x1, Pallas kernels, per_device(): pl.pallas_call(hand_on, out_shape=tuple((jax.ShapeDtypeStruct(x.shape, x....  2.45 us

profile of v4, /device:TPU:9, one launch (start us, length us, event | category | flops | bytes accessed | tf_op | source)
XLA Modules:
  0.0 59.8 jit_solution(7282411420422351824)
XLA Ops:
  0.6 56.7 %shard_map.120 = (bf16[128,2,16,128]{3,2,1,0:T(8,128)(2,1)}, bf16[512,128]{1,0:T(8,128)(2,1)}, bf16[512,128]{1,0:T(8,128)(2,1)}, bf16[64,2560]{1,0:T(8,128)(2,1)}) custom-call(s32[8]{0:T(128)} %len_ref.1, bf16[512,128]{1,0:T(8,128)(2,1)} %bitcast.6, bf16[512,128]{1,0:T(8,128)(2,1)} %bitcast.7, bf16[128,128]{1,0:T(8,128)(2,1)} %bitcast.8, ...), custom_call_target="tpu_custom_call" | custom-call | tf_op jit(solution)/shard_map/pallas_call | solution.py:603
  57.4 2.5 %shard_map.121 = (bf16[128,2,16,128]{3,2,1,0:T(8,128)(2,1)}, bf16[512,128]{1,0:T(8,128)(2,1)}, bf16[512,128]{1,0:T(8,128)(2,1)}, bf16[64,2560]{1,0:T(8,128)(2,1)}) custom-call(bf16[128,2,16,128]{3,2,1,0:T(8,128)(2,1)} %get-tuple-element.12.refs_0_, bf16[512,128]{1,0:T(8,128)(2,1)} %get-tuple-element.13.refs_1_, bf16[512,128]{1,0:T(8,128)(2,1)} %get-tuple-element.14.refs_2_, ...), custom_call_target="tpu_custom_call" | custom-call | tf_op jit(solution)/shard_map/pallas_call | solution.py:628

commit v5 on v4

--- a/solution.py
+++ b/solution.py
@@ -48,11 +48,11 @@
     cotts,
     kv_all,
     pr_all,
-    s_buf,
-    dp_buf,
-    m_ref,
-    l_ref,
-    d_ref,
+    kcat,
+    vcat,
+    kcat_t,
+    dk_acc,
+    dv_acc,
     dq_acc,
     own,
     gsend,
@@ -244,45 +244,44 @@
         return pr_all[:, :, which, lax.rem(pair, H)].reshape(prompt_keys, E)
 
     def block(j):
-        return pl.ds(pl.multiple_of(j * L, L), L)
-
-    prompt_rows = pl.ds(n * L, prompt_keys)
-
-    def stats(pair, where, k, v, diag):
-        s = dot_nn(k, qts[pair]) * log_scale
-        if diag:
-            key = lax.broadcasted_iota(jnp.int32, s.shape, 0)
-            query = lax.broadcasted_iota(jnp.int32, s.shape, 1) // F
-            s = jnp.where(key <= query, s, masked_score)
-        dp = dot_nn(v, cotts[pair])
-        s_buf[where, :] = s
-        dp_buf[where, :] = dp
-        top = jnp.max(s, axis=0, keepdims=True)
-        if diag:
-            e = jnp.exp2(s - top)
-            l_ref[...] = jnp.sum(e, axis=0, keepdims=True)
-            d_ref[...] = jnp.sum(e * dp, axis=0, keepdims=True)
-            m_ref[...] = top
-        else:
-            m_old = m_ref[...]
-            m_new = jnp.maximum(m_old, top)
-            e = jnp.exp2(s - m_new)
-            a = jnp.exp2(m_old - m_new)
-            l_ref[...] = l_ref[...] * a + jnp.sum(e, axis=0, keepdims=True)
-            d_ref[...] = d_ref[...] * a + jnp.sum(e * dp, axis=0, keepdims=True)
-            m_ref[...] = m_new
-
-    def grads(pair, where, k, first=False):
-        prob = jnp.exp2(s_buf[where, :] - m_ref[...])
-        ds = (prob * (dp_buf[where, :] - d_ref[...])).astype(jnp.bfloat16)
-        dv = dot_nn(prob.astype(jnp.bfloat16), cots[pair])
-        dk = dot_nn(ds, qs[pair]) * scale
-        term = dot_nn(k.T, ds)
-        if first:
-            dq_acc[pair] = term
-        else:
-            dq_acc[pair] += term
+        return pl.ds(pl.multiple_of(prompt_keys + j * L, L), L)
+
+    wide_rows = 256 if rows % 512 == 0 else rows
+    abreast = 2 if rows % 512 == 0 else 1
+
+    def query_block(i, c, b, keys):
+        cols = pl.ds(pl.multiple_of(b * wide_rows, wide_rows), wide_rows)
+        q_t, cot_t = qts[i, :, cols], cotts[i, :, cols]
+        s = dot_nn(kcat[:keys], q_t) * log_scale
+        key = lax.broadcasted_iota(jnp.int32, (L, wide_rows), 0)
+        query = (lax.broadcasted_iota(jnp.int32, (L, wide_rows), 1) + b * wide_rows) // F
+        last = jnp.where(key <= query, s[keys - L :], masked_score)
+        s = jnp.concatenate([s[: keys - L], last], axis=0)
+        e = jnp.exp2(s - jnp.max(s, axis=0, keepdims=True))
+        inverse = 1.0 / jnp.sum(e, axis=0, keepdims=True)
+        dp = dot_nn(vcat[:keys], cot_t)
+        prob = e * inverse
+        weighted = prob * dp
+        delta = jnp.sum(weighted, axis=0, keepdims=True)
+        ds = (weighted - prob * delta).astype(jnp.bfloat16)
+        dv = dot_nn(prob.astype(jnp.bfloat16), cots[i, cols])
+        dk = dot_nn(ds, qs[i, cols])
+        dq_acc[i, :, cols] = dot_nn(kcat_t[:, :keys], ds)
         return dk, dv
+
+    def whole_pair(i, c):
+        keys = prompt_keys + (c + 1) * L
+        kcat_t[:, :keys] = kcat[:keys].T
+        dk_acc[:keys] = jnp.zeros((keys, E), jnp.float32)
+        dv_acc[:keys] = jnp.zeros((keys, E), jnp.float32)
+
+        def some(b, carry):
+            terms = [query_block(i, c, b * abreast + k, keys) for k in range(abreast)]
+            dk_acc[:keys] += functools.reduce(lambda x, y: x + y, [x[0] for x in terms])
+            dv_acc[:keys] += functools.reduce(lambda x, y: x + y, [x[1] for x in terms])
+            return carry
+
+        lax.fori_loop(0, rows // (wide_rows * abreast), some, 0)
 
     def grad_copy(j, i):
         return remote(gsend.at[j, i], grecv.at[j, i], g_send.at[j, i], g_recv.at[j, i], at(pp=down))
@@ -330,27 +329,32 @@
 
         pass_on(step + 1)
         send_own(step + 2)
-        stats(i, block(p), kv_ref[i, 0], kv_ref[i, 1], True)
-        stats(i, prompt_rows, prompt_block(0, i), prompt_block(1, i), False)
-
-        def chunk_stats(o, inner):
+        kcat[:prompt_keys] = prompt_block(0, i)
+        vcat[:prompt_keys] = prompt_block(1, i)
+        kcat[block(p), :] = kv_ref[i, 0]
+        vcat[block(p), :] = kv_ref[i, 1]
+
+        def place(o, inner):
             j = p - o
 
             @pl.when(p == n - 1)
             def _():
                 chunk_wait(j, i)
 
-            stats(i, block(j), kv_all[j, i, 0], kv_all[j, i, 1], False)
+            kcat[block(j), :] = kv_all[j, i, 0]
+            vcat[block(j), :] = kv_all[j, i, 1]
             return inner
 
-        lax.fori_loop(1, p + 1, chunk_stats, 0)
-        d_ref[...] = d_ref[...] / l_ref[...]
-        m_ref[...] = m_ref[...] + jnp.log(l_ref[...]) * log2_e
+        lax.fori_loop(1, p + 1, place, 0)
+        for c in range(n):
+
+            @pl.when(p == c)
+            def _():
+                whole_pair(i, c)
 
         h = lax.rem(i, H)
-        dk, dv = grads(i, prompt_rows, prompt_block(0, i), True)
-        dk = dk.reshape(n, G, piece, E)
-        dv = dv.reshape(n, G, piece, E)
+        dk = (dk_acc[:prompt_keys] * scale).reshape(n, G, piece, E)
+        dv = dv_acc[:prompt_keys].reshape(n, G, piece, E)
         for gg in range(G):
             pacc[gg, :, 0, h] += dk[:, gg]
             pacc[gg, :, 1, h] += dv[:, gg]
@@ -362,9 +366,8 @@
                 r1(o).start()
 
         def chunk_grads(j, inner):
-            dk, dv = grads(i, block(j), kv_all[j, i, 0])
-            gsend[j, i, 0] = dk.astype(jnp.bfloat16)
-            gsend[j, i, 1] = dv.astype(jnp.bfloat16)
+            gsend[j, i, 0] = (dk_acc[block(j), :] * scale).astype(jnp.bfloat16)
+            gsend[j, i, 1] = dv_acc[block(j), :].astype(jnp.bfloat16)
 
             @pl.when(p == n - 1)
             def _():
@@ -373,6 +376,8 @@
             return inner
 
         lax.fori_loop(0, p, chunk_grads, 0)
+        own[i, 0] = dk_acc[block(p), :] * scale
+        own[i, 1] = dv_acc[block(p), :]
 
         @pl.when(step == pairs - 1)
         def _():
@@ -385,10 +390,6 @@
             ps2[...] = total.astype(jnp.bfloat16)
             for o in range(1, n):
                 r2(o).start()
-
-        dk, dv = grads(i, block(p), kv_ref[i, 0])
-        own[i, 0] = dk
-        own[i, 1] = dv
 
         @pl.when((lag > 0) & (step >= lag))
         def _():
@@ -559,11 +560,11 @@
         pltpu.VMEM((pairs, E, rows), bf16),
         pltpu.VMEM((n, pairs, 2, L, E), bf16),
         pltpu.VMEM((n, G, 2, H, piece, E), bf16),
-        pltpu.VMEM((n * L + n * prompt_rows, rows), f32),
-        pltpu.VMEM((n * L + n * prompt_rows, rows), f32),
-        pltpu.VMEM((1, rows), f32),
-        pltpu.VMEM((1, rows), f32),
-        pltpu.VMEM((1, rows), f32),
+        pltpu.VMEM((n * (L + prompt_rows), E), bf16),
+        pltpu.VMEM((n * (L + prompt_rows), E), bf16),
+        pltpu.VMEM((E, n * (L + prompt_rows)), bf16),
+        pltpu.VMEM((n * (L + prompt_rows), E), f32),
+        pltpu.VMEM((n * (L + prompt_rows), E), f32),
         pltpu.VMEM((pairs, E, rows), f32),
         pltpu.VMEM((pairs, 2, L, E), f32),
         pltpu.VMEM((n, pairs, 2, L, E), bf16),

time: 60 us -> 64.6 us (1.077)
  Pallas kernels: 59.2 us -> 63.8 us
    pallas_call x1, Pallas kernels: 56.7 us -> 61.4 us  [per_device(): pl.pallas_call(functools.partial(kernel, sizes), out_shape=(jax.ShapeDtyp...]
where the time goes in v5:
time: 64.6 us; the launch traced here: 64.5 us
  Pallas kernels  63.8 us (99%)
    pallas_call x1, Pallas kernels, per_device(): pl.pallas_call(functools.partial(kernel, sizes), out_shape=(jax.ShapeDtyp...  61.4 us
    pallas_call x1, Pallas kernels, per_device(): pl.pallas_call(hand_on, out_shape=tuple((jax.ShapeDtypeStruct(x.shape, x....  2.45 us

profile of v5, /device:TPU:9, one launch (start us, length us, event | category | flops | bytes accessed | tf_op | source)
XLA Modules:
  0.0 64.5 jit_solution(5524744400641613908)
XLA Ops:
  0.6 61.4 %shard_map.120 = (bf16[128,2,16,128]{3,2,1,0:T(8,128)(2,1)}, bf16[512,128]{1,0:T(8,128)(2,1)}, bf16[512,128]{1,0:T(8,128)(2,1)}, bf16[64,2560]{1,0:T(8,128)(2,1)}) custom-call(s32[8]{0:T(128)} %len_ref.1, bf16[512,128]{1,0:T(8,128)(2,1)} %bitcast.6, bf16[512,128]{1,0:T(8,128)(2,1)} %bitcast.7, bf16[128,128]{1,0:T(8,128)(2,1)} %bitcast.8, ...), custom_call_target="tpu_custom_call" | custom-call | tf_op jit(solution)/shard_map/pallas_call | solution.py:604
  62.0 2.5 %shard_map.121 = (bf16[128,2,16,128]{3,2,1,0:T(8,128)(2,1)}, bf16[512,128]{1,0:T(8,128)(2,1)}, bf16[512,128]{1,0:T(8,128)(2,1)}, bf16[64,2560]{1,0:T(8,128)(2,1)}) custom-call(bf16[128,2,16,128]{3,2,1,0:T(8,128)(2,1)} %get-tuple-element.12.refs_0_, bf16[512,128]{1,0:T(8,128)(2,1)} %get-tuple-element.13.refs_1_, bf16[512,128]{1,0:T(8,128)(2,1)} %get-tuple-element.14.refs_2_, ...), custom_call_target="tpu_custom_call" | custom-call | tf_op jit(solution)/shard_map/pallas_call | solution.py:629

commit v6 on v4

--- a/solution.py
+++ b/solution.py
@@ -234,6 +234,10 @@
                 prompt_a_wait(o)
                 for oo in range(1, G):
                     prompt_b(o, oo).start()
+            pass_on(0)
+            send_own(2)
+    pass_on(1)
+    send_own(3)
     for o in range(1, n):
         for oo in range(1, G):
             prompt_b_wait(o, oo)
@@ -324,12 +328,8 @@
     def one_pair(step, carry):
         i = order(step)
 
-        @pl.when(step == 0)
-        def _():
-            pass_on(0)
-
-        pass_on(step + 1)
-        send_own(step + 2)
+        pass_on(step + 2)
+        send_own(step + 4)
         stats(i, block(p), kv_ref[i, 0], kv_ref[i, 1], True)
         stats(i, prompt_rows, prompt_block(0, i), prompt_block(1, i), False)
 
@@ -425,7 +425,7 @@
 
     for o in range(1, G):
         r3(o).start()
-    lax.fori_loop(left, jnp.where(p > 0, pairs, left), add_rest, 0)
+    lax.fori_loop(left, jnp.where(p >= n - 2, pairs, left), add_rest, 0)
     for r in range(R):
         write_query_grad(r)
     out_copy.start()
@@ -451,6 +451,7 @@
         xs[o - 1] = project(peer(t, o, T)).astype(jnp.bfloat16)
         x_copy(o).start()
     opart[...] = project(t)
+    lax.fori_loop(left, jnp.where((p > 0) & (p < n - 2), pairs, left), add_rest, 0)
 
     result = opart[...]
     for o in range(1, T):
@@ -468,7 +469,7 @@
 
     for o in range(1, G):
         o_copy(o).start()
-    lax.fori_loop(left, jnp.where(p > 0, left, pairs), add_rest, 0)
+    lax.fori_loop(left, jnp.where((p > 0) | (n < 2), left, pairs), add_rest, 0)
     for which, ref in enumerate((dkey_ref, dvalue_ref)):
         for i in range(pairs):
             wide[which, pl.ds(i, L, stride=pairs), :] = own[i, which]

time: 60 us -> 57.2 us (0.953)
  the two profiles are of different devices: /device:TPU:9 before, /device:TPU:1 now
where the time goes in v6:
time: 57.2 us; the launch traced here: 57 us
  Pallas kernels  56.4 us (99%)
  between operations  0.64 us (1%)
    pallas_call x1, Pallas kernels, per_device(): pl.pallas_call(functools.partial(kernel, sizes), out_shape=(jax.ShapeDtyp...  53.9 us
    pallas_call x1, Pallas kernels, per_device(): pl.pallas_call(hand_on, out_shape=tuple((jax.ShapeDtypeStruct(x.shape, x....  2.45 us

profile of v6, /device:TPU:1, one launch (start us, length us, event | category | flops | bytes accessed | tf_op | source)
XLA Modules:
  0.0 57.0 jit_solution(7506042333115581684)
XLA Ops:
  0.6 53.9 %shard_map.120 = (bf16[128,2,16,128]{3,2,1,0:T(8,128)(2,1)}, bf16[512,128]{1,0:T(8,128)(2,1)}, bf16[512,128]{1,0:T(8,128)(2,1)}, bf16[64,2560]{1,0:T(8,128)(2,1)}) custom-call(s32[8]{0:T(128)} %len_ref.1, bf16[512,128]{1,0:T(8,128)(2,1)} %bitcast.6, bf16[512,128]{1,0:T(8,128)(2,1)} %bitcast.7, bf16[128,128]{1,0:T(8,128)(2,1)} %bitcast.8, ...), custom_call_target="tpu_custom_call" | custom-call | tf_op jit(solution)/shard_map/pallas_call | solution.py:604
  54.6 2.5 %shard_map.121 = (bf16[128,2,16,128]{3,2,1,0:T(8,128)(2,1)}, bf16[512,128]{1,0:T(8,128)(2,1)}, bf16[512,128]{1,0:T(8,128)(2,1)}, bf16[64,2560]{1,0:T(8,128)(2,1)}) custom-call(bf16[128,2,16,128]{3,2,1,0:T(8,128)(2,1)} %get-tuple-element.12.refs_0_, bf16[512,128]{1,0:T(8,128)(2,1)} %get-tuple-element.13.refs_1_, bf16[512,128]{1,0:T(8,128)(2,1)} %get-tuple-element.14.refs_2_, ...), custom_call_target="tpu_custom_call" | custom-call | tf_op jit(solution)/shard_map/pallas_call | solution.py:629

commit v7 on v6

--- a/solution.py
+++ b/solution.py
@@ -223,12 +223,13 @@
         q = q_ref[:, r].astype(jnp.float32)
         c = cot_ref[:, r].astype(jnp.float32)
         for h in range(H):
-            part = q[:, h * F : (h + 1) * F].reshape(rows, E)
-            qs[r * H + h] = part.astype(jnp.bfloat16)
-            qts[r * H + h] = part.T.astype(jnp.bfloat16)
-            live = jnp.where(pos < length, c[:, h * F : (h + 1) * F], 0.0).reshape(rows, E)
-            cots[r * H + h] = live.astype(jnp.bfloat16)
-            cotts[r * H + h] = live.T.astype(jnp.bfloat16)
+            part = q[:, h * F : (h + 1) * F].reshape(rows, E).astype(jnp.bfloat16)
+            qs[r * H + h] = part
+            qts[r * H + h] = part.T
+            live = jnp.where(pos < length, c[:, h * F : (h + 1) * F], 0.0)
+            live = live.reshape(rows, E).astype(jnp.bfloat16)
+            cots[r * H + h] = live
+            cotts[r * H + h] = live.T
         if r == 0:
             for o in range(1, n):
                 prompt_a_wait(o)
@@ -408,6 +409,7 @@
 
     left = jnp.maximum(pairs - lag, 0)
 
+    write_query_grad(0)
     for o in range(1, n):
         r2_wait(o)
     total = pacc[g, p]
@@ -426,7 +428,7 @@
     for o in range(1, G):
         r3(o).start()
     lax.fori_loop(left, jnp.where(p >= n - 2, pairs, left), add_rest, 0)
-    for r in range(R):
+    for r in range(1, R):
         write_query_grad(r)
     out_copy.start()
     for copy in weight_copies():
@@ -506,12 +508,20 @@
         x_copy(o).wait_send()
 
 
+hand_parts = 4
+
+
 def hand_on(*refs):
     count = 4
     sources, targets, held = refs[:count], refs[count : 2 * count], refs[2 * count : 3 * count]
     in_sem, out_sem = refs[3 * count :]
-    arriving = [pltpu.make_async_copy(sources[i], held[i], in_sem.at[i]) for i in range(count)]
-    leaving = [pltpu.make_async_copy(held[i], targets[i], out_sem.at[i]) for i in range(count)]
+    arriving, leaving = [], []
+    for i in range(count):
+        part = sources[i].shape[0] // hand_parts
+        for k in range(hand_parts):
+            here = pl.ds(k * part, part)
+            arriving.append(pltpu.make_async_copy(sources[i].at[here], held[i].at[here], in_sem.at[i, k]))
+            leaving.append(pltpu.make_async_copy(held[i].at[here], targets[i].at[here], out_sem.at[i, k]))
     for copy in arriving:
         copy.start()
     for came, goes in zip(arriving, leaving):
@@ -631,7 +641,7 @@
         out_shape=tuple(jax.ShapeDtypeStruct(x.shape, x.dtype) for x in results),
         in_specs=[anywhere] * 4,
         out_specs=(anywhere,) * 4,
-        scratch_shapes=[pltpu.VMEM(x.shape, x.dtype) for x in results] + [dma((4,)), dma((4,))],
+        scratch_shapes=[pltpu.VMEM(x.shape, x.dtype) for x in results] + [dma((4, hand_parts)), dma((4, hand_parts))],
         compiler_params=pltpu.CompilerParams(vmem_limit_bytes=60 * 1024 * 1024),
     )(*results)
     shape = response_key.shape

time: 57.2 us -> 57.1 us (level)
  no operation moved by 1% of the time
where the time goes in v7:
time: 57.1 us; the launch traced here: 57 us
  Pallas kernels  56.3 us (99%)
  between operations  0.64 us (1%)
    pallas_call x1, Pallas kernels, per_device(): pl.pallas_call(functools.partial(kernel, sizes), out_shape=(jax.ShapeDtyp...  53.9 us
    pallas_call x1, Pallas kernels, per_device(): pl.pallas_call(hand_on, out_shape=tuple((jax.ShapeDtypeStruct(x.shape, x....  2.38 us

profile of v7, /device:TPU:1, one launch (start us, length us, event | category | flops | bytes accessed | tf_op | source)
XLA Modules:
  0.0 57.0 jit_solution(16427104649739559935)
XLA Ops:
  0.6 53.9 %shard_map.120 = (bf16[128,2,16,128]{3,2,1,0:T(8,128)(2,1)}, bf16[512,128]{1,0:T(8,128)(2,1)}, bf16[512,128]{1,0:T(8,128)(2,1)}, bf16[64,2560]{1,0:T(8,128)(2,1)}) custom-call(s32[8]{0:T(128)} %len_ref.1, bf16[512,128]{1,0:T(8,128)(2,1)} %bitcast.6, bf16[512,128]{1,0:T(8,128)(2,1)} %bitcast.7, bf16[128,128]{1,0:T(8,128)(2,1)} %bitcast.8, ...), custom_call_target="tpu_custom_call" | custom-call | tf_op jit(solution)/shard_map/pallas_call | solution.py:614
  54.6 2.4 %shard_map.121 = (bf16[128,2,16,128]{3,2,1,0:T(8,128)(2,1)}, bf16[512,128]{1,0:T(8,128)(2,1)}, bf16[512,128]{1,0:T(8,128)(2,1)}, bf16[64,2560]{1,0:T(8,128)(2,1)}) custom-call(bf16[128,2,16,128]{3,2,1,0:T(8,128)(2,1)} %get-tuple-element.12.refs_0_, bf16[512,128]{1,0:T(8,128)(2,1)} %get-tuple-element.13.refs_1_, bf16[512,128]{1,0:T(8,128)(2,1)} %get-tuple-element.14.refs_2_, ...), custom_call_target="tpu_custom_call" | custom-call | tf_op jit(solution)/shard_map/pallas_call | solution.py:639
